TPU v7x, 32 devices: a whole 2x2x4 slice. The times are simulated.
32 devices in a mesh: head: 4 (over x, core), seq: 8 (over z, y).
Axes of the slice: x: 2, y: 2, z: 4, core: 2. Of those that a mesh axis runs over, the one named last changes fastest.
Arguments:
- x_input: bfloat16 [8192, 16384], P('seq', 'head'), may hold values from -5 to 5
- bc_input: bfloat16 [2, 8192, 1024], P(None, 'seq', 'head'), may hold values from -5 to 5
- dt_input: bfloat16 [8192, 128], P('seq', 'head'), may hold values from -8 to 256
- z_gate: bfloat16 [8192, 16384], P('seq', 'head'), may hold values from -400 to 400
- conv_x: float32 [4, 16384], P(None, 'head'), may hold values from -2 to 2
- conv_bc: float32 [2, 4, 1024], P(None, None, 'head'), may hold values from -2 to 2
- dt_bias: float32 [128], P('head'), may hold values from -0.3 to 0.3
- a_log: float32 [128], P('head'), may hold values from -10 to 1
- d_skip: float32 [128], P('head'), may hold values from 0.5 to 1.5
- init_state: float32 [128, 128, 128], P('head'), may hold values from -5 to 5
- norm_gain: float32 [16384], P('head'), may hold values from 0.5 to 1.5
Outputs:
- normed: bfloat16 [8192, 16384], P('seq', 'head')
All inputs are finite; a program needn't handle non-finite values.
Results may differ from a plain program's by a relative error of at most 0.0034.
Values may be sent and summed in bfloat16 or wider, within the bound.
A program may use at most 128 MiB of HBM per device.

v0:
```python
import jax
import jax.numpy as jnp
from jax import lax
from jax.sharding import PartitionSpec as P

SPAN = 256
INNER = 16384


norm_eps = 1e-05


def from_behind(value, axis, by):
    length = lax.axis_size(axis)
    pairs = [(i, i + by) for i in range(length) if 0 <= i + by < length]
    return lax.ppermute(value, axis, pairs)


def combine_states(earlier, later):
    return (earlier[0] * later[0], later[0][..., None, None] * earlier[1] + later[1])


def prefix_sources(pieces):
    inclusive = lax.associative_scan(combine_states, pieces, axis=0)
    return jnp.concatenate([jnp.zeros_like(pieces[1][:1]), inclusive[1][:-1]], axis=0)


def local(
    x_input,
    bc_input,
    dt_input,
    z_gate,
    conv_x,
    conv_bc,
    dt_bias,
    a_log,
    d_skip,
    init_state,
    norm_gain,
):
    row_count = x_input.shape[0]
    channels = x_input.shape[1]
    heads_here = a_log.shape[0]
    head_dim = init_state.shape[1]
    state_dim = init_state.shape[2]
    groups_here = bc_input.shape[2] // state_dim
    group_heads = heads_here // groups_here
    segment_len = SPAN
    segments = row_count // segment_len
    rim_rows = conv_x.shape[0] - 1
    x_rim, bc_rim = from_behind(
        (x_input[row_count - rim_rows :], bc_input[:, row_count - rim_rows :]), "seq", 1
    )
    x_full = jnp.concatenate([x_rim, x_input], axis=0)
    bc_full = jnp.concatenate([bc_rim, bc_input], axis=1)
    x_sum = jnp.zeros((row_count, channels), jnp.float32)
    bc_sum = jnp.zeros(bc_input.shape, jnp.float32)
    for tap_index in range(rim_rows + 1):
        x_sum = x_sum + conv_x[tap_index] * x_full[tap_index : tap_index + row_count]
        bc_sum = (
            bc_sum
            + conv_bc[:, tap_index][:, None, :] * bc_full[:, tap_index : tap_index + row_count]
        )
    x_conv = jax.nn.silu(x_sum).astype(jnp.bfloat16)
    bc_conv = jax.nn.silu(bc_sum).astype(jnp.bfloat16)
    b_mat = bc_conv[0].reshape(segments, segment_len, groups_here, state_dim)
    c_mat = bc_conv[1].reshape(segments, segment_len, groups_here, state_dim)
    time_step = jax.nn.softplus(dt_input.astype(jnp.float32) + dt_bias).reshape(
        segments, segment_len, heads_here
    )
    log_cum = jnp.cumsum(-jnp.exp(a_log) * time_step, axis=1)
    scores = jnp.einsum("clgn,csgn->cgls", c_mat, b_mat, preferred_element_type=jnp.float32)
    cum_heads = jnp.transpose(log_cum, (0, 2, 1))
    step_heads = jnp.transpose(time_step, (0, 2, 1))
    log_gap = cum_heads[:, :, :, None] - cum_heads[:, :, None, :]
    causal = jnp.arange(segment_len)[:, None] >= jnp.arange(segment_len)[None, :]
    weights = (
        jnp.where(causal, jnp.exp(jnp.where(causal, log_gap, 0.0)), 0.0) * step_heads[:, :, None, :]
    )
    mixing = (
        scores[:, :, None]
        * weights.reshape(segments, groups_here, group_heads, segment_len, segment_len)
    ).astype(jnp.bfloat16)
    x_heads = x_conv.reshape(segments, segment_len, groups_here, group_heads, head_dim)
    local_part = jnp.einsum(
        "cghls,csghp->clghp", mixing, x_heads, preferred_element_type=jnp.float32
    )
    tail_weight = jnp.exp(log_cum[:, -1:, :] - log_cum) * time_step
    x_weighted = (
        x_heads * tail_weight.reshape(segments, segment_len, groups_here, group_heads, 1)
    ).astype(jnp.bfloat16)
    block_state = jnp.einsum(
        "clghp,clgn->cghpn", x_weighted, b_mat, preferred_element_type=jnp.float32
    )
    block_decay = jnp.exp(log_cum[:, -1, :]).reshape(segments, groups_here, group_heads)
    running = jnp.zeros((groups_here, group_heads, head_dim, state_dim), jnp.float32)
    factor = jnp.ones((groups_here, group_heads), jnp.float32)
    starts = []
    factors = []
    for piece_index in range(segments):
        starts.append(running)
        factors.append(factor)
        running = block_decay[piece_index][..., None, None] * running + block_state[piece_index]
        factor = factor * block_decay[piece_index]
    is_first = lax.axis_index("seq") == 0
    seed_state = init_state.reshape(groups_here, group_heads, head_dim, state_dim)
    summary = running + jnp.where(is_first, factor[..., None, None] * seed_state, 0.0)
    source_count = lax.axis_size("seq")
    per_piece = heads_here // source_count
    flat_states = summary.reshape(source_count, per_piece, head_dim, state_dim)
    piece_decays = factor.reshape(source_count, per_piece)
    ordered = prefix_sources(
        (
            lax.all_to_all(piece_decays, "seq", split_axis=0, concat_axis=0, tiled=True),
            lax.all_to_all(flat_states, "seq", split_axis=0, concat_axis=0, tiled=True),
        )
    )
    prefix = lax.all_to_all(ordered, "seq", split_axis=0, concat_axis=0, tiled=True).reshape(
        groups_here, group_heads, head_dim, state_dim
    )
    incoming = prefix + jnp.where(is_first, seed_state, 0.0)
    start_states = jnp.stack(starts) + jnp.stack(factors)[..., None, None] * incoming
    state_low = start_states.astype(jnp.bfloat16)
    carried_part = jnp.exp(log_cum).reshape(
        segments, segment_len, groups_here, group_heads, 1
    ) * jnp.einsum("clgn,cghpn->clghp", c_mat, state_low, preferred_element_type=jnp.float32)
    skip_part = d_skip.reshape(groups_here, group_heads, 1) * x_heads
    mixed_out = (local_part + carried_part + skip_part).reshape(row_count, channels)
    gated_out = mixed_out * jax.nn.silu(z_gate.astype(jnp.float32))
    square_sum = jnp.sum(gated_out * gated_out, axis=1)
    total_square = lax.psum(square_sum, "head")
    inverse_rms = lax.rsqrt(total_square / INNER + norm_eps)
    return (gated_out * inverse_rms[:, None] * norm_gain).astype(jnp.bfloat16)


def solution(mesh):
    placed = (
        P("seq", "head"),
        P(None, "seq", "head"),
        P("seq", "head"),
        P("seq", "head"),
        P(None, "head"),
        P(None, None, "head"),
        P("head"),
        P("head"),
        P("head"),
        P("head", None, None),
        P("head"),
    )
    return jax.shard_map(
        local, mesh=mesh, in_specs=placed, out_specs=P("seq", "head"), check_vma=False
    )
```

profile of v0, /device:TPU:27, one launch (start us, length us, event | category | flops | bytes accessed | tf_op | source)
XLA Modules:
  0.0 321.6 jit_solution(15686120314785858558)
XLA Ops:
  0.0 0.7 slice.173
  0.7 3.1 collective-permute-start.1
  3.8 0.9 slice.165
  4.7 1.9 collective-permute-start
  6.6 1.0 compare_select_fusion
  7.7 0.7 exponential_negate_fusion
  8.6 2.3 reduce-window.6
  12.0 0.7 mul.461
  12.7 5.7 %all-to-all-start.1 = ((f32[8,1,4]{2,1,0:T(1,128)}), f32[8,1,4]{2,1,0:T(1,128)}, u32[]{:S(2)}, u32[]{:S(2)}) async-start(f32[8,1,4]{2,1,0:T(1,128)} %bitcast.18), calls=%async_computation.1 | async-start | bytes 8192 | tf_op jit(solution)/shard_map/all_to_all | solution.py:114
  18.4 0.9 fusion.46
  19.3 0.8 fusion.41
  20.0 1.1 fusion.45
  22.7 0.6 mul.432
  23.3 0.7 mul.435
  24.0 3.5 %multiply_convert_fusion.6 = bf16[2,1024,256]{2,1,0:T(8,128)(2,1)S(1)} fusion(bf16[2,1024,256]{2,1,0:T(8,128)(2,1)} %param.12, bf16[2,3,256]{2,1,0:T(4,128)(2,1)S(1)} %collective-permute-done.1, f32[2,256]{1,0:T(2,128)S(1)} %get-tuple-element.41, f32[2,256]{1,0:T(2,128)S(1)} %get-tuple-element.42, f32[2,256]{1,0:T(2,128)S(1)} %get-tuple-element.43, ...), kind=kLoop, calls=%fused_computation.41 | loop fusion | flops 13107200 | bytes 2108416 | tf_op jit(solution)/shard_map/convert_element_type | solution.py:65
  27.5 0.9 fusion.43
  28.5 18.9 %fusion.20 = bf16[128,8,32,128]{3,1,2,0:T(8,128)(2,1)} fusion(bf16[1024,4096]{1,0:T(8,128)(2,1)} %param.11, f32[4096]{0:T(1024)S(1)} %bitcast.98, bf16[3,4096]{1,0:T(4,128)(2,1)S(1)} %collective-permute-done, f32[4096]{0:T(1024)S(1)} %bitcast.99, f32[4096]{0:T(1024)S(1)} %bitcast.97, f32[4096]{0:T(1024)S(1)} %bitcast.96), kind=kLoop, calls=%fused_computation.32 | loop fusion | flops 104857600 | bytes 16867328
  47.4 9.4 %copy.115 = bf16[128,8,32,128]{3,2,1,0:T(8,128)(2,1)} copy(bf16[128,8,32,128]{3,1,2,0:T(8,128)(2,1)} %fusion.20) | data formatting | bytes 16777216
  56.8 13.7 %copy.89 = bf16[4,256,2,16,128]{1,4,3,2,0:T(8,128)(2,1)} copy(bf16[4,256,2,16,128]{4,3,2,1,0:T(8,128)(2,1)} %bitcast.83) | data formatting | bytes 16777216 | tf_op jit(solution)/shard_map/reshape | solution.py:84
  70.6 5.7 %fusion.16 = f32[4,2,16,128,128]{4,3,2,1,0:T(8,128)S(1)} fusion(bf16[4,256,2,16,128]{1,4,3,2,0:T(8,128)(2,1)} %copy.89, f32[4,256,2,16]{1,3,2,0:T(8,128)S(1)} %bitcast.94, bf16[4,256,2,128,1]{3,2,1,0,4:T(2,128)(2,1)S(1)} %bitcast.91), kind=kOutput, calls=%fused_computation.27 | convolution fusion | flops 1086324736 | bytes 17432576 | tf_op jit(solution)/shard_map/clghp,clgn->cghpn/dot_general | solution.py:92
  76.3 6.3 %multiply_add_fusion = (f32[1,2,16,128,128]{4,3,2,1,0:T(8,128)}, f32[1,2,16,128,128]{4,3,2,1,0:T(8,128)}, f32[1,2,16,128,128]{4,3,2,1,0:T(8,128)}, f32[1,2,16,12...) fusion(f32[2,16]{1,0:T(2,128)S(1)} %copy-done.13, ...), kind=kLoop, calls=%fused_computation.39 | loop fusion | flops 2621440 | bytes 23069056 | tf_op jit(solution)/shard_map/add | solution.py:103
  82.7 6.2 %select_add_fusion = f32[8,4,128,128]{3,2,1,0:T(8,128)} fusion(f32[8,4,128,128]{3,2,1,0:T(8,128)} %bitcast.89, f32[8,4,128,128]{3,2,1,0:T(8,128)} %bitcast.88, f32[8,4,128,128]{3,2,1,0:T(8,128)} %bitcast.87, f32[8,4,128,128]{3,2,1,0:T(8,128)} %bitcast.86, f32[8,4,128,128]{3,2,1,0:T(8,128)} %bitcast.85, f32[8,4]{1,0:T(8,128)S(1)} %copy-done.6, ...), kind=kLoop, calls=%fused_computation.38 | loop fusion | flops 5242880 | bytes 12583553 | tf_op jit(solution)/shard_map/add | solution.py:107
  88.9 5.4 %all-to-all-start = ((f32[8,4,128,128]{3,2,1,0:T(8,128)}), f32[8,4,128,128]{3,2,1,0:T(8,128)S(1)}, u32[]{:S(2)}, u32[]{:S(2)}) async-start(f32[8,4,128,128]{3,2,1,0:T(8,128)} %select_add_fusion), calls=%async_computation | async-start | bytes 4194304 | tf_op jit(solution)/shard_map/all_to_all | solution.py:115
  94.4 0.8 copy.95
  96.2 44.7 %all-to-all-done = f32[8,4,128,128]{3,2,1,0:T(8,128)S(1)} async-done(((f32[8,4,128,128]{3,2,1,0:T(8,128)}), f32[8,4,128,128]{3,2,1,0:T(8,128)S(1)}, u32[]{:S(2)}, u32[]{:S(2)}) %all-to-all-start) | async-done | bytes 2097184 | tf_op jit(solution)/shard_map/all_to_all | solution.py:115
  141.3 0.8 pad_add_fusion
  142.2 0.8 pad_maximum_fusion.3
  143.0 3.5 %pad.22 = f32[4,4,128,128]{3,2,1,0:T(8,128)S(1)} pad(f32[2,4,128,128]{3,2,1,0:T(8,128)} %pad_maximum_fusion.3, f32[]{:T(128)} %constant.9.clone.1), padding=0_1_1x0_0_0x0_0_0x0_0_0 | pad | bytes 1572868 | tf_op jit(solution)/shard_map/pad | solution.py:24
  146.5 5.7 %pad.23 = f32[4,4,128,128]{3,2,1,0:T(8,128)} pad(f32[2,4,128,128]{3,2,1,0:T(8,128)} %pad_add_fusion, f32[]{:T(128)} %constant.9.clone.1), padding=1_0_1x0_0_0x0_0_0x0_0_0 | pad | bytes 1572868 | tf_op jit(solution)/shard_map/pad | solution.py:24
  152.2 2.3 add.159
  154.6 10.1 %pad.114 = f32[8,4,128,128]{3,2,1,0:T(8,128)} pad(f32[4,4,128,128]{3,2,1,0:T(8,128)} %add.159, f32[]{:T(128)} %constant.9.clone.1), padding=1_0_1x0_0_0x0_0_0x0_0_0 | pad | bytes 3145732
  164.7 1.3 fusion.28
  166.4 1.7 slice_add_fusion.3
  168.1 1.6 concatenate.19
  169.7 5.5 %all-to-all-start.2 = ((f32[8,4,128,128]{3,2,1,0:T(8,128)}), f32[8,4,128,128]{3,2,1,0:T(8,128)}, u32[]{:S(2)}, u32[]{:S(2)}) async-start(f32[8,4,128,128]{3,2,1,0:T(8,128)} %concatenate.19), calls=%async_computation.2 | async-start | bytes 4194304 | tf_op jit(solution)/shard_map/all_to_all | solution.py:118
  176.0 0.6 iota_compare_fusion
  176.7 1.6 broadcast_select_fusion
  178.2 1.2 reshape_squeeze.6
  179.4 1.8 fusion.31
  181.2 41.4 %all-to-all-done.2 = f32[8,4,128,128]{3,2,1,0:T(8,128)} async-done(((f32[8,4,128,128]{3,2,1,0:T(8,128)}), f32[8,4,128,128]{3,2,1,0:T(8,128)}, u32[]{:S(2)}, u32[]{:S(2)}) %all-to-all-start.2) | async-done | bytes 2097184 | tf_op jit(solution)/shard_map/all_to_all | solution.py:118
  222.6 2.6 bitcast_add_fusion
  225.3 10.5 %fusion.21 = f32[4,2,16,128,256]{4,3,2,1,0:T(8,128)} fusion(f32[1,2,16,128,128]{4,3,2,1,0:T(8,128)S(1)} %copy-done, f32[1,2,16,128,128]{4,3,2,1,0:T(8,128)} %get-tuple-element.14, f32[1,2,16,128,128]{4,3,2,1,0:T(8,128)} %get-tuple-element.15, f32[4]{0:T(128)S(1)} %pad.35.clone, f32[2,16,128,128]{3,2,1,0:T(8,128)S(1)} %bitcast_add_fusion, ...), kind=kOutput, calls=%fused_computation.33 | convolution fusion | flops 1086324736 | bytes 25690640 | tf_op jit(solution)/shard_map/clgn,cghpn->clghp/dot_general | solution.py:126
  235.8 17.5 %fusion.2 = f32[4,256,2,16,128]{1,4,3,2,0:T(8,128)} fusion(bf16[4,256,2,16,128]{1,4,3,2,0:T(8,128)(2,1)S(1)} %bitcast.82, f32[4,2,16,128,256]{4,3,2,1,0:T(8,128)} %fusion.21, f32[4,2,16,256]{3,2,1,0:T(8,128)S(1)} %copy.88, f32[4,2,16,256]{3,2,1,0:T(8,128)S(1)} %reduce_window_sum.27, f32[4,2,256,256]{3,2,1,0:T(8,128)} %fusion.31, ...), kind=kOutput, calls=%fused_computation.7 | convolution fusion | flops 2218786816 | bytes 44499072 | tf_op jit(solution)/shard_map/cghls,csghp->clghp/dot_general | solution.py:85
  253.3 19.9 %copy.100 = f32[4,256,2,16,128]{4,3,2,1,0:T(8,128)} copy(f32[4,256,2,16,128]{1,4,3,2,0:T(8,128)} %fusion.2) | data formatting | bytes 33554432 | tf_op jit(solution)/shard_map/add | solution.py:128
  273.2 18.2 %reshape.230 = f32[1024,4096]{1,0:T(8,128)} reshape(f32[4,256,2,16,128]{4,3,2,1,0:T(8,128)} %copy.100) | data formatting | bytes 33554432 | tf_op jit(solution)/shard_map/reshape | solution.py:128
  291.4 10.7 %multiply_reduce_fusion = f32[1024]{0:T(1024)S(1)} fusion(f32[1024,4096]{1,0:T(8,128)} %reshape.230, bf16[1024,4096]{1,0:T(8,128)(2,1)} %param.14), kind=kLoop, calls=%fused_computation.15 | loop fusion | flops 33553408 | bytes 25169920 | tf_op jit(solution)/shard_map/reduce_sum | solution.py:130
  302.1 5.5 %psum.7 = f32[1024]{0:T(1024)S(1)} all-reduce(f32[1024]{0:T(1024)S(1)} %multiply_reduce_fusion), channel_id=1, replica_groups=mesh['head'=4,'seq'=8] {'head'}, use_global_device_ids=true, to_apply=%region_3.4 | all-reduce | flops 1024 | bytes 8192 | tf_op jit(solution)/shard_map/psum | solution.py:131
  307.7 13.9 %multiply_convert_fusion.2 = bf16[1024,4096]{1,0:T(8,128)(2,1)} fusion(f32[4096]{0:T(1024)S(1)} %copy-done.5, f32[1024]{0:T(1024)S(1)} %add_rsqrt_fusion, f32[1024,4096]{1,0:T(8,128)} %reshape.230, bf16[1024,4096]{1,0:T(8,128)(2,1)} %param.14), kind=kLoop, calls=%fused_computation.14 | loop fusion | flops 37748736 | bytes 33574912 | tf_op jit(solution)/shard_map/convert_element_type | solution.py:133
  (94 shorter events, 5.8 us)
Async XLA Ops:
  0.7 23.3 %collective-permute-start.1 = (bf16[2,3,256]{2,1,0:T(4,128)(2,1)S(1)}, bf16[2,3,256]{2,1,0:T(4,128)(2,1)S(1)}, u32[]{:S(2)}, u32[]{:S(2)}) collective-permute-start(bf16[2,3,256]{2,1,0:T(4,128)(2,1)S(1)} %slice.173), channel_id=1, source_target_pairs={{0,1},{1,2},{2,3},{3,4},{4,5},{5,6},{6,7},{8,9},{9,10},{10,11},{11... | collective-permute-start | bytes 9224 | tf_op jit(solution)/shard_map/ppermute | solution.py:16
  4.7 23.8 %collective-permute-start = (bf16[3,4096]{1,0:T(4,128)(2,1)S(1)}, bf16[3,4096]{1,0:T(4,128)(2,1)S(1)}, u32[]{:S(2)}, u32[]{:S(2)}) collective-permute-start(bf16[3,4096]{1,0:T(4,128)(2,1)S(1)} %slice.165), channel_id=1, source_target_pairs={{0,1},{1,2},{2,3},{3,4},{4,5},{5,6},{6,7},{8,9},{9,10},{10,11},{11... | collective-permute-start | bytes 73736 | tf_op jit(solution)/shard_map/ppermute | solution.py:16
  12.0 9.4 %copy-start.7 = (f32[32]{0:T(128)}, f32[32]{0:T(128)S(1)}, u32[]{:S(2)}) copy-start(f32[32]{0:T(128)S(1)} %get-tuple-element.40) | copy-start | bytes 388
  12.0 9.4 %copy-start.9 = (f32[32]{0:T(128)}, f32[32]{0:T(128)S(1)}, u32[]{:S(2)}) copy-start(f32[32]{0:T(128)S(1)} %get-tuple-element.38) | copy-start | bytes 388
  12.7 76.2 %all-to-all-start.1 = ((f32[8,1,4]{2,1,0:T(1,128)}), f32[8,1,4]{2,1,0:T(1,128)}, u32[]{:S(2)}, u32[]{:S(2)}) async-start(f32[8,1,4]{2,1,0:T(1,128)} %bitcast.18), calls=%async_computation.1 | async-start | bytes 8192 | tf_op jit(solution)/shard_map/all_to_all | solution.py:114
  28.5 42.1 %copy-start.1 = (bf16[4,256,2,128]{3,2,1,0:T(2,128)(2,1)}, bf16[4,256,2,128]{3,2,1,0:T(2,128)(2,1)S(1)}, u32[]{:S(2)}) copy-start(bf16[4,256,2,128]{3,2,1,0:T(2,128)(2,1)S(1)} %reshape_squeeze.7) | copy-start | bytes 1572868
  70.5 5.8 %copy-start.11 = (f32[2,16]{1,0:T(2,128)S(1)}, f32[2,16]{1,0:T(2,128)}, u32[]{:S(2)}) copy-start(f32[2,16]{1,0:T(2,128)} %mul.426) | copy-start | bytes 388
  70.5 5.8 %copy-start.12 = (f32[2,16]{1,0:T(2,128)S(1)}, f32[2,16]{1,0:T(2,128)}, u32[]{:S(2)}) copy-start(f32[2,16]{1,0:T(2,128)} %mul.432) | copy-start | bytes 388
  70.6 5.8 %copy-start.13 = (f32[2,16]{1,0:T(2,128)S(1)}, f32[2,16]{1,0:T(2,128)}, u32[]{:S(2)}) copy-start(f32[2,16]{1,0:T(2,128)} %mul.435) | copy-start | bytes 388
  76.3 6.4 %copy-start.6 = (f32[8,4]{1,0:T(8,128)S(1)}, f32[8,4]{1,0:T(8,128)}, u32[]{:S(2)}) copy-start(f32[8,4]{1,0:T(8,128)} %get-tuple-element.37) | copy-start | bytes 388
  88.9 52.0 %all-to-all-start = ((f32[8,4,128,128]{3,2,1,0:T(8,128)}), f32[8,4,128,128]{3,2,1,0:T(8,128)S(1)}, u32[]{:S(2)}, u32[]{:S(2)}) async-start(f32[8,4,128,128]{3,2,1,0:T(8,128)} %select_add_fusion), calls=%async_computation | async-start | bytes 4194304 | tf_op jit(solution)/shard_map/all_to_all | solution.py:115
  166.1 9.2 %copy-start.10 = (f32[32]{0:T(128)S(1)}, f32[32]{0:T(128)}, u32[]{:S(2)}) copy-start(f32[32]{0:T(128)} %copy-done.9) | copy-start | bytes 388
  166.1 9.2 %copy-start.8 = (f32[32]{0:T(128)S(1)}, f32[32]{0:T(128)}, u32[]{:S(2)}) copy-start(f32[32]{0:T(128)} %copy-done.7) | copy-start | bytes 388
  166.1 9.3 %copy-start.14 = (f32[32]{0:T(128)S(1)}, f32[32]{0:T(128)}, u32[]{:S(2)}) copy-start(f32[32]{0:T(128)} %get-tuple-element.5) | copy-start | bytes 388
  166.1 9.8 %copy-start.15 = (f32[32]{0:T(128)S(1)}, f32[32]{0:T(128)}, u32[]{:S(2)}) copy-start(f32[32]{0:T(128)} %param.19) | copy-start | bytes 388
  168.1 11.3 %copy-start.2 = (bf16[4,256,2,128]{3,2,1,0:T(2,128)(2,1)S(1)}, bf16[4,256,2,128]{3,2,1,0:T(2,128)(2,1)}, u32[]{:S(2)}) copy-start(bf16[4,256,2,128]{3,2,1,0:T(2,128)(2,1)} %copy-done.1) | copy-start | bytes 1572868
  169.7 52.9 %all-to-all-start.2 = ((f32[8,4,128,128]{3,2,1,0:T(8,128)}), f32[8,4,128,128]{3,2,1,0:T(8,128)}, u32[]{:S(2)}, u32[]{:S(2)}) async-start(f32[8,4,128,128]{3,2,1,0:T(8,128)} %concatenate.19), calls=%async_computation.2 | async-start | bytes 4194304 | tf_op jit(solution)/shard_map/all_to_all | solution.py:118
  175.2 50.0 %copy-start = (f32[1,2,16,128,128]{4,3,2,1,0:T(8,128)S(1)}, f32[1,2,16,128,128]{4,3,2,1,0:T(8,128)}, u32[]{:S(2)}) copy-start(f32[1,2,16,128,128]{4,3,2,1,0:T(8,128)} %get-tuple-element.13) | copy-start | bytes 6291460
  222.6 13.2 %slice-start = ((s8[8388608]{0:T(1024)(128)(4,1)}), s8[4194304]{0:T(1024)(128)(4,1)S(1)}, s32[]{:S(2)}) async-start(s8[8388608]{0:T(1024)(128)(4,1)} %bitcast.81), calls=%async_computation.3 | async-start | bytes 8388608
  225.3 10.5 %slice-start.1 = ((s8[8388608]{0:T(1024)(128)(4,1)}), s8[4194304]{0:T(1024)(128)(4,1)S(1)}, s32[]{:S(2)}) async-start(s8[8388608]{0:T(1024)(128)(4,1)} %bitcast.81), calls=%async_computation.4 | async-start | bytes 8388608
  225.3 10.5 %copy-start.3 = (f32[4,256,32]{1,2,0:T(8,128)S(1)}, f32[4,256,32]{1,2,0:T(8,128)}, u32[]{:S(2)}) copy-start(f32[4,256,32]{1,2,0:T(8,128)} %get-tuple-element.26) | copy-start | bytes 393220
  225.3 10.5 %copy-start.4 = (pred[256,256]{1,0:T(8,128)(4,1)S(1)}, pred[256,256]{1,0:T(8,128)(4,1)}, u32[]{:S(2)}) copy-start(pred[256,256]{1,0:T(8,128)(4,1)} %iota_compare_fusion) | copy-start | bytes 196612
  291.4 16.3 %copy-start.5 = (f32[4096]{0:T(1024)S(1)}, f32[4096]{0:T(1024)}, u32[]{:S(2)}) copy-start(f32[4096]{0:T(1024)} %param.21) | copy-start | bytes 49156
where the time goes:
time: 328 us; the launch traced here: 322 us
  local copies, waits for them, and re-layouts  94.1 us (29%)
  waiting for transfers between devices  86.1 us (26%)
  other arithmetic  78.3 us (24%)
  matrix products  35.5 us (11%)
  starting transfers between devices  21.7 us (7%)
  blocking collectives  5.52 us (2%)
    all_to_all x1, waiting for transfers between devices, local(): lax.all_to_all(flat_states, 'seq', split_axis=0, concat_axis=0, tiled=True)  44.7 us
    all_to_all x1, waiting for transfers between devices, local(): lax.all_to_all(ordered, 'seq', split_axis=0, concat_axis=0, tiled=True)  41.4 us
    add x1, local copies, waits for them, and re-layouts, local(): local_part + carried_part + skip_part  19.9 us
    unnamed x40, local copies, waits for them, and re-layouts  19.6 us
    unnamed x2, other arithmetic  18.9 us
    reshape x1, local copies, waits for them, and re-layouts, local(): (local_part + carried_part + skip_part).reshape(row_count, channels)  18.2 us
    dot_general x1, matrix products, local(): jnp.einsum('cghls,csghp->clghp', mixing, x_heads, preferred_element_type=...  17.5 us
    convert_element_type x1, other arithmetic, local(): return (gated_out * inverse_rms[:, None] * norm_gain).astype(jnp.bfloat16)  13.9 us
  transfers between devices with their start and end apart: 5, of which 2 were waited for; matrix products, arithmetic and copies ran while one was open for 26% of the time, Pallas kernels for 0%

commit v1 on v0

v1 whole, which is shorter than its diff:
```python
import functools

import jax
import jax.numpy as jnp
from jax import lax
from jax.experimental import pallas as pl
from jax.experimental.pallas import tpu as pltpu
from jax.sharding import PartitionSpec as P

SPAN = 256
STEP_HEADS = 4
LANES = 128
LOG2E = 1.4426950408889634
norm_eps = 1e-05
VMEM = 56 * 1024 * 1024
f32 = jnp.float32
bf16 = jnp.bfloat16


def dot(a, b):
    return jnp.dot(a, b, preferred_element_type=f32)


def half_silu(h):
    return h + h * jnp.tanh(h)


def conv_half(halo, block, taps):
    full = jnp.concatenate([halo, block], axis=0)
    acc = block * taps[3:4]
    for back in range(1, 4):
        acc = acc + pltpu.roll(full, back, 0)[8:] * taps[3 - back : 4 - back]
    return acc


def prepare_kernel(dt_ref, bias_ref, alog_ref, bc_ref, rim_ref, taps_ref,
                   cols_ref, vrow_ref, dec_ref, c_ref, bt_ref):
    rows = dt_ref.shape[0]
    segments = rows // SPAN
    r = lax.broadcasted_iota(jnp.int32, (SPAN, SPAN), 0)
    c = lax.broadcasted_iota(jnp.int32, (SPAN, SPAN), 1)
    tri = (r >= c).astype(f32)
    lane = lax.broadcasted_iota(jnp.int32, (SPAN, LANES), 1) // (LANES // 4)
    rate = -jnp.exp(alog_ref[...]) * LOG2E
    pre = jnp.zeros((1, LANES), f32)
    decays = []
    for k in range(segments):
        at = slice(k * SPAN, (k + 1) * SPAN)
        v = dt_ref[at].astype(f32) + bias_ref[...]
        ts = jnp.maximum(v, 0.0) + jnp.log1p(jnp.exp(-jnp.abs(v)))
        cum = jnp.dot(tri, ts * rate, precision=lax.Precision.HIGHEST,
                      preferred_element_type=f32)
        end = cum[SPAN - 1 : SPAN]
        vrow_ref[:, at] = (cum - jnp.log2(ts)).T[: LANES // 4]
        tail = jnp.exp2(end - cum) * ts
        cols_ref[at] = jnp.where(
            lane == 0, cum,
            jnp.where(lane == 1, jnp.exp2(cum),
                      jnp.where(lane == 2, tail, jnp.exp2(cum + pre))))
        decays.append(jnp.exp2(end))
        pre = pre + end
    decays.append(jnp.exp2(pre))
    decays.append(jnp.zeros((8 - len(decays), LANES), f32))
    dec_ref[...] = jnp.concatenate(decays, axis=0)
    for i in range(2):
        taps = taps_ref[i] * 0.5
        halo = rim_ref[i]
        for k in range(segments):
            at = slice(k * SPAN, (k + 1) * SPAN)
            block = bc_ref[i, at].astype(f32)
            out = half_silu(conv_half(halo, block, taps))
            halo = block[SPAN - 8 :]
            if i == 0:
                bt_ref[:, at] = out.T.astype(bf16)
            else:
                c_ref[at] = out.astype(bf16)


def turned(ref_value, width=LANES):
    step = pl.program_id(0)
    return pltpu.roll(ref_value, lax.rem(LANES - step * STEP_HEADS, LANES), 1)


def states_kernel(x_ref, rim_ref, taps_ref, cols_ref, dec_ref, bt_ref,
                  xc_ref, starts_ref, sum_ref, halo_ref, turn_ref):
    rows = x_ref.shape[0]
    segments = rows // SPAN
    turn_ref[...] = turned(cols_ref[...])
    dec = turned(dec_ref[...])
    halo_ref[...] = rim_ref[...]
    running = None
    for k in range(segments):
        at = slice(k * SPAN, (k + 1) * SPAN)
        weighted = []
        for j in range(STEP_HEADS):
            lanes = slice(j * LANES, (j + 1) * LANES)
            block = x_ref[at, lanes].astype(f32)
            if k == 0:
                halo = halo_ref[:, lanes]
            else:
                halo = x_ref[k * SPAN - 16 : k * SPAN, lanes].astype(f32)[8:]
            xc = half_silu(conv_half(halo, block, taps_ref[:, lanes] * 0.5)).astype(bf16)
            xc_ref[at, lanes] = xc
            tail = turn_ref[at, 64 + j : 65 + j]
            weighted.append((xc.astype(f32) * tail).astype(bf16))
        fresh = dot(bt_ref[:, at], jnp.concatenate(weighted, axis=1))
        nxt = []
        for j in range(STEP_HEADS):
            piece = fresh[:, j * LANES : (j + 1) * LANES]
            if k > 0:
                starts_ref[k - 1, :, j * LANES : (j + 1) * LANES] = running[j].astype(bf16)
                piece = piece + dec[k : k + 1, j : j + 1] * running[j]
            nxt.append(piece)
        running = nxt
    for j in range(STEP_HEADS):
        sum_ref[j] = running[j].astype(sum_ref.dtype)


def local_kernel(xc_ref, cols_ref, vrow_ref, c_ref, bt_ref, starts_ref, skip_ref,
                 out_ref, turn_ref):
    rows = xc_ref.shape[0]
    segments = rows // SPAN
    half = SPAN // 2
    turn_ref[...] = turned(cols_ref[...])
    r = lax.broadcasted_iota(jnp.int32, (half, half), 0)
    c = lax.broadcasted_iota(jnp.int32, (half, half), 1)
    causal = r >= c
    for k in range(segments):
        base = k * SPAN
        at = slice(base, base + SPAN)
        top, low = slice(base, base + half), slice(base + half, base + SPAN)
        scores = dot(c_ref[at], bt_ref[:, at])
        s_tt = jnp.where(causal, scores[:half, :half], 0.0)
        s_lt = scores[half:, :half]
        s_ll = jnp.where(causal, scores[half:, half:], 0.0)
        if k > 0:
            carried = dot(c_ref[at], starts_ref[k - 1])
        for j in range(STEP_HEADS):
            lanes = slice(j * LANES, (j + 1) * LANES)
            u = turn_ref[at, j : j + 1]
            v = vrow_ref[0, j : j + 1, at]
            m_tt = s_tt * jnp.exp2(jnp.minimum(u[:half] - v[:, :half], 100.0))
            m_lt = s_lt * jnp.exp2(u[half:] - v[:, :half])
            m_ll = s_ll * jnp.exp2(jnp.minimum(u[half:] - v[:, half:], 100.0))
            x = xc_ref[at, lanes]
            y_t = dot(m_tt.astype(bf16), x[:half])
            y_l = dot(jnp.concatenate([m_lt, m_ll], axis=1).astype(bf16), x)
            y = jnp.concatenate([y_t, y_l], axis=0) + skip_ref[:, lanes] * x.astype(f32)
            if k > 0:
                y = y + turn_ref[at, 32 + j : 33 + j] * carried[:, lanes]
            out_ref[at, lanes] = y


def gate_kernel(part_ref, z_ref, cols_ref, c_ref, inc_ref, out_ref, sq_ref):
    cols = turned(cols_ref[...])
    rows = part_ref.shape[0]

    @pl.when(pl.program_id(0) == 0)
    def _():
        sq_ref[...] = jnp.zeros_like(sq_ref)

    for k in range(rows // SPAN):
        at = slice(k * SPAN, (k + 1) * SPAN)
        total = sq_ref[at]
        for j in range(STEP_HEADS):
            lanes = slice(j * LANES, (j + 1) * LANES)
            carried = dot(c_ref[at], inc_ref[j])
            mixed = part_ref[at, lanes] + cols[at, 96 + j : 97 + j] * carried
            gated = mixed * half_silu(z_ref[at, lanes].astype(f32) * 0.5)
            total = total + gated * gated
            out_ref[at, lanes] = gated.astype(out_ref.dtype)
        sq_ref[at] = total


def local(x_input, bc_input, dt_input, z_gate, conv_x, conv_bc, dt_bias, a_log,
          d_skip, init_state, norm_gain, *, inner):
    rows, channels = x_input.shape
    heads = a_log.shape[0]
    state = init_state.shape[2]
    groups = bc_input.shape[2] // state
    steps = heads // STEP_HEADS
    per_group = steps // groups
    width = STEP_HEADS * LANES
    segments = rows // SPAN
    n = lax.axis_size("seq")
    me = lax.axis_index("seq")
    group_cols = bc_input.shape[2]

    tail = jnp.concatenate(
        [x_input[rows - 8 :], bc_input[0, rows - 8 :], bc_input[1, rows - 8 :]], axis=1)
    rim = lax.ppermute(tail, "seq", [(i, i + 1) for i in range(n - 1)]).astype(f32)
    x_rim = rim[:, :channels]
    bc_rim = jnp.stack([rim[:, channels : channels + group_cols], rim[:, channels + group_cols :]])

    params = functools.partial(pltpu.CompilerParams, vmem_limit_bytes=VMEM)
    four = lambda a: jnp.concatenate([a] * 4, axis=-1)
    cols, vrow, dec, c_mat, b_t = pl.pallas_call(
        prepare_kernel,
        out_shape=(
            jax.ShapeDtypeStruct((rows, LANES), f32),
            jax.ShapeDtypeStruct((heads, rows), f32),
            jax.ShapeDtypeStruct((8, LANES), f32),
            jax.ShapeDtypeStruct((rows, group_cols), bf16),
            jax.ShapeDtypeStruct((group_cols, rows), bf16),
        ),
        compiler_params=params(),
        name="prepare",
    )(four(dt_input), four(dt_bias)[None], four(a_log)[None], bc_input, bc_rim, conv_bc)
    vrow = vrow.reshape(steps, STEP_HEADS, rows)

    whole = lambda shape: pl.BlockSpec(shape, lambda i: (0,) * len(shape))
    stripe = pl.BlockSpec((rows, width), lambda i: (0, i))
    bt_spec = pl.BlockSpec((state, rows), lambda i: (i // per_group, 0))
    c_spec = pl.BlockSpec((rows, state), lambda i: (0, i // per_group))
    cols_spec = whole((rows, LANES))
    starts_spec = pl.BlockSpec((segments - 1, state, width), lambda i: (0, 0, i))
    heads_spec = pl.BlockSpec((STEP_HEADS, state, LANES), lambda i: (i, 0, 0))
    x_conv, starts, summary = pl.pallas_call(
        states_kernel,
        grid=(steps,),
        in_specs=[stripe, pl.BlockSpec((8, width), lambda i: (0, i)),
                  pl.BlockSpec((4, width), lambda i: (0, i)), cols_spec, whole((8, LANES)), bt_spec],
        out_specs=(stripe, starts_spec, heads_spec),
        out_shape=(
            jax.ShapeDtypeStruct((rows, channels), bf16),
            jax.ShapeDtypeStruct((segments - 1, state, channels), bf16),
            jax.ShapeDtypeStruct((heads, state, LANES), bf16),
        ),
        scratch_shapes=[pltpu.VMEM((8, width), f32), pltpu.VMEM((rows, LANES), f32)],
        compiler_params=params(),
        name="states",
    )(x_input, x_rim, conv_x, cols, dec, b_t)

    partial = pl.pallas_call(
        local_kernel,
        grid=(steps,),
        in_specs=[stripe, cols_spec, pl.BlockSpec((1, STEP_HEADS, rows), lambda i: (i, 0, 0)),
                  c_spec, bt_spec, starts_spec, pl.BlockSpec((1, width), lambda i: (0, i))],
        out_specs=stripe,
        out_shape=jax.ShapeDtypeStruct((rows, channels), f32),
        scratch_shapes=[pltpu.VMEM((rows, LANES), f32)],
        compiler_params=params(),
        cost_estimate=pl.CostEstimate(flops=8 * 10**9, bytes_accessed=40 * 2**20, transcendentals=0),
        name="inside",
    )(x_conv, cols, vrow, c_mat, b_t, starts, jnp.repeat(d_skip, LANES)[None])

    factor = lax.all_gather(dec[segments, :heads], "seq", axis=0)
    share = heads // n
    got = lax.all_to_all(summary, "seq", split_axis=0, concat_axis=0, tiled=True)
    got = got.reshape(n, share, state, LANES).astype(f32)
    mine = lax.dynamic_slice_in_dim(factor, me * share, share, 1)[:, :, None, None]
    seed = lax.dynamic_slice_in_dim(init_state, me * share, share, 0).transpose(0, 2, 1)
    running = seed
    sent = []
    for i in range(n):
        sent.append(running.astype(bf16))
        running = mine[i] * running + got[i]
    incoming = lax.all_to_all(jnp.concatenate(sent, axis=0), "seq", split_axis=0, concat_axis=0,
                              tiled=True)

    gated, squares = pl.pallas_call(
        gate_kernel,
        grid=(steps,),
        in_specs=[stripe, stripe, cols_spec, c_spec, heads_spec],
        out_specs=(stripe, cols_spec),
        out_shape=(jax.ShapeDtypeStruct((rows, channels), f32),
                   jax.ShapeDtypeStruct((rows, LANES), f32)),
        compiler_params=params(),
        name="gate",
    )(partial, z_gate, cols, c_mat, incoming)
    total = lax.psum(jnp.sum(squares, axis=1), "head")
    inverse = lax.rsqrt(total / inner + norm_eps)
    return (gated * inverse[:, None] * norm_gain).astype(bf16)


def solution(mesh):
    placed = (
        P("seq", "head"), P(None, "seq", "head"), P("seq", "head"), P("seq", "head"),
        P(None, "head"), P(None, None, "head"), P("head"), P("head"), P("head"),
        P("head", None, None), P("head"),
    )

    def run(*args):
        return jax.shard_map(
            functools.partial(local, inner=args[0].shape[1]),
            mesh=mesh, in_specs=placed, out_specs=P("seq", "head"), check_vma=False,
        )(*args)

    return run
```

time: 328 us -> 144 us (0.44)
  the two profiles are of different devices: /device:TPU:27 before, /device:TPU:0 now
where the time goes in v1:
time: 144 us; the launch traced here: 143 us
  Pallas kernels  60.1 us (42%)
  blocking collectives  35 us (24%)
  other arithmetic  20.2 us (14%)
  starting transfers between devices  16.4 us (11%)
  local copies, waits for them, and re-layouts  6.62 us (5%)
  waiting for transfers between devices  4.98 us (3%)
    all_gather x1, blocking collectives, local(): factor = lax.all_gather(dec[segments, :heads], 'seq', axis=0)  29.4 us
    pallas_call x1, Pallas kernels, local(): pl.pallas_call(gate_kernel, grid=(steps,), in_specs=[stripe, stripe, cols...  19.6 us
    pallas_call x1, Pallas kernels, local(): pl.pallas_call(states_kernel, grid=(steps,), in_specs=[stripe, pl.BlockSp...  18.4 us
    pallas_call x1, Pallas kernels, local(): pl.pallas_call(local_kernel, grid=(steps,), in_specs=[stripe, cols_spec,...  16.7 us
    convert_element_type x1, other arithmetic, local(): return (gated * inverse[:, None] * norm_gain).astype(bf16)  9.73 us
    all_to_all x1, starting transfers between devices, local(): lax.all_to_all(jnp.concatenate(sent, axis=0), 'seq', split_axis=0, concat...  6.2 us
    psum x1, blocking collectives, local(): total = lax.psum(jnp.sum(squares, axis=1), 'head')  5.67 us
    pallas_call x1, Pallas kernels, local(): pl.pallas_call(prepare_kernel, out_shape=(jax.ShapeDtypeStruct((rows, LAN...  5.32 us
  transfers between devices with their start and end apart: 3, of which 1 were waited for; matrix products, arithmetic and copies ran while one was open for 4% of the time, Pallas kernels for 12%

profile of v1, /device:TPU:0, one launch (start us, length us, event | category | flops | bytes accessed | tf_op | source)
XLA Modules:
  0.0 143.4 jit_solution(2510685112397260474)
XLA Ops:
  0.0 0.0 copy-start
  0.0 0.9 slice_bitcast_fusion.3
  0.9 0.8 slice.77
  1.7 4.9 %collective-permute-start = (bf16[8,4608]{1,0:T(8,128)(2,1)S(1)}, bf16[8,4608]{1,0:T(8,128)(2,1)S(1)}, u32[]{:S(2)}, u32[]{:S(2)}) collective-permute-start(bf16[8,4608]{1,0:T(8,128)(2,1)S(1)} %pad_maximum_fusion.1), channel_id=1, source_target_pairs={{0,1},{1,2},{2,3},{3,4},{4,5},{5,6},{6,7},{8,9},{9,10},{10,11},{11... | collective-permute-start | bytes 221192 | tf_op jit(solution)/shard_map/ppermute | solution.py:191
  6.6 1.0 copy.17
  7.6 1.0 pad_maximum_fusion.dt_ref
  8.6 1.5 %maximum_bitcast_fusion = (f32[1,128]{1,0:T(1,128)}, f32[1,128]{1,0:T(1,128)}) fusion(f32[32]{0:T(128)} %param.17, f32[32]{0:T(128)} %param.18), kind=kLoop, calls=%fused_computation.40 | loop fusion | flops 768 | bytes 1280 | tf_op jit(solution)/shard_map/broadcast_in_dim | solution.py:208
  10.1 0.0 collective-permute-done
  10.1 0.6 pad_maximum_fusion.2.rim_ref
  10.7 5.3 %prepare.1 = (f32[1024,128]{1,0:T(8,128)}, f32[32,1024]{1,0:T(8,128)}, f32[8,128]{1,0:T(8,128)}, bf16[1024,256]{1,0:T(8,128)(2,1)}, bf16[256,1024]{1,0:T(8,128)(2,1)}) custom-call(bf16[1024,128]{1,0:T(8,128)(2,1)} %pad_maximum_fusion.dt_ref, f32[1,128]{1,0:T(1,128)} %get-tuple-element.42.bias_ref, f32[1,128]{1,0:T(1,128)} %get-tuple-element.43.alog_ref, ...), custom_call_target="tpu_custom_call" | custom-call | tf_op jit(solution)/shard_map/prepare/pallas_call | solution.py:197
  16.0 0.7 slice.105.rim_ref
  16.7 18.4 %states.1 = (bf16[1024,4096]{1,0:T(8,128)(2,1)}, bf16[3,128,4096]{2,1,0:T(8,128)(2,1)}, bf16[32,128,128]{2,1,0:T(8,128)(2,1)}) custom-call(bf16[1024,4096]{1,0:T(8,128)(2,1)} %x_ref.1, f32[8,4096]{1,0:T(8,128)} %slice.105.rim_ref, f32[4,4096]{1,0:T(4,128)} %taps_ref.3, f32[1024,128]{1,0:T(8,128)} %get-tuple-element.15.cols_ref, ...), custom_call_target="tpu_custom_call" | custom-call | tf_op jit(solution)/shard_map/states/pallas_call | solution.py:218
  35.1 0.0 copy-start.3
  35.1 0.0 copy-start.5
  35.2 5.3 %all-to-all-start = ((bf16[32,128,128]{2,1,0:T(8,128)(2,1)}), bf16[32,128,128]{2,1,0:T(8,128)(2,1)S(1)}, u32[]{:S(2)}, u32[]{:S(2)}) async-start(bf16[32,128,128]{2,1,0:T(8,128)(2,1)} %get-tuple-element.22), calls=%async_computation | async-start | bytes 2097152 | tf_op jit(solution)/shard_map/all_to_all | solution.py:249
  40.4 0.0 copy-done
  40.5 0.1 copy.22
  40.6 0.7 bitcast_dynamic-update-slice_fusion
  41.3 0.7 slice_bitcast_fusion.4
  42.0 29.4 %all-gather = f32[8,1,32]{2,1,0:T(1,128)S(1)} all-gather(f32[1,1,32]{2,1,0:T(1,128)S(1)} %slice_bitcast_fusion.4), channel_id=1, replica_groups=mesh['head'=4,'seq'=8] {'seq'}, dimensions={0}, use_global_device_ids=true | all-gather | bytes 1152 | tf_op jit(solution)/shard_map/all_gather | solution.py:247
  71.3 0.1 fusion.2
  71.4 0.0 all-to-all-done
  71.4 0.2 convert_element_type.40
  71.7 0.7 convert_dynamic-update-slice_fusion.5
  72.4 0.8 convert_dynamic-update-slice_fusion.4
  73.2 0.7 convert_dynamic-update-slice_fusion.3
  73.9 0.8 convert_dynamic-update-slice_fusion.2
  74.7 0.8 convert_dynamic-update-slice_fusion.1
  75.4 0.8 convert_dynamic-update-slice_fusion
  76.2 0.7 fusion.1
  76.9 6.2 %all-to-all-start.1 = ((bf16[32,128,128]{2,1,0:T(8,128)(2,1)}), bf16[32,128,128]{2,1,0:T(8,128)(2,1)S(1)}, u32[]{:S(2)}, u32[]{:S(2)}) async-start(bf16[32,128,128]{2,1,0:T(8,128)(2,1)} %fusion.1), calls=%async_computation.1 | async-start | bytes 2097152 | tf_op jit(solution)/shard_map/all_to_all | solution.py:258
  83.1 0.0 copy-done.3
  83.1 0.7 reshape.42.vrow_ref
  83.8 0.0 copy-done.5
  83.8 0.7 broadcast_in_dim.14
  84.5 16.7 %inside.1.part_ref = f32[1024,4096]{1,0:T(8,128)} custom-call(bf16[1024,4096]{1,0:T(8,128)(2,1)} %get-tuple-element.18.xc_ref, f32[1024,128]{1,0:T(8,128)} %get-tuple-element.15.cols_ref, f32[8,4,1024]{2,1,0:T(4,128)} %reshape.42.vrow_ref, bf16[1024,256]{1,0:T(8,128)(2,1)} %get-tuple-element.20.c_ref, bf16[256,1024]{1,0:T(8,128)(2,1)} %get-tuple-element.17.bt_ref, ...), custom_call_target="tpu_custom_call" | custom-call | flops 8000000000 | bytes 41943040 | tf_op jit(solution)/shard_map/inside/pallas_call | solution.py:234
  101.1 0.0 copy-start.4
  101.1 5.0 %all-to-all-done.1.inc_ref = bf16[32,128,128]{2,1,0:T(8,128)(2,1)S(1)} async-done(((bf16[32,128,128]{2,1,0:T(8,128)(2,1)}), bf16[32,128,128]{2,1,0:T(8,128)(2,1)S(1)}, u32[]{:S(2)}, u32[]{:S(2)}) %all-to-all-start.1) | async-done | bytes 1048608 | tf_op jit(solution)/shard_map/all_to_all | solution.py:258
  106.1 0.0 copy-start.2
  106.1 1.0 copy-done.2
  107.1 19.6 %gate.1 = (f32[1024,4096]{1,0:T(8,128)}, f32[1024,128]{1,0:T(8,128)}) custom-call(f32[1024,4096]{1,0:T(8,128)} %inside.1.part_ref, bf16[1024,4096]{1,0:T(8,128)(2,1)} %z_ref.1, f32[1024,128]{1,0:T(8,128)} %get-tuple-element.15.cols_ref, bf16[1024,256]{1,0:T(8,128)(2,1)} %get-tuple-element.20.c_ref, bf16[32,128,128]{2,1,0:T(8,128)(2,1)} %copy-done.2), custom_call_target="tpu_custom_call" | custom-call | tf_op jit(solution)/shard_map/gate/pallas_call | solution.py:261
  126.7 1.2 reduce_sum.9
  128.0 5.7 %psum.7 = f32[1024]{0:T(1024)S(1)} all-reduce(f32[1024]{0:T(1024)S(1)} %reduce_sum.9), channel_id=1, replica_groups=mesh['head'=4,'seq'=8] {'head'}, use_global_device_ids=true, to_apply=%region_1.0 | all-reduce | flops 1024 | bytes 8192 | tf_op jit(solution)/shard_map/psum | solution.py:271
  133.7 0.0 copy-start.1
  133.7 0.0 copy-done.4
  133.7 9.7 %multiply_convert_fusion = bf16[1024,4096]{1,0:T(8,128)(2,1)} fusion(f32[1024,4096]{1,0:T(8,128)} %get-tuple-element.23, f32[4096]{0:T(1024)S(1)} %copy-done.4, f32[1024]{0:T(1024)S(1)} %add_rsqrt_fusion), kind=kLoop, calls=%fused_computation | loop fusion | flops 12582912 | bytes 25186304 | tf_op jit(solution)/shard_map/convert_element_type | solution.py:273
  143.4 0.0 copy-done.1
  (5 shorter events, 0.1 us)
Async XLA Ops:
  0.0 40.4 %copy-start = (f32[32,128,128]{2,1,0:T(8,128)S(1)}, f32[32,128,128]{2,1,0:T(8,128)}, u32[]{:S(2)}) copy-start(f32[32,128,128]{2,1,0:T(8,128)} %param.20) | copy-start | bytes 6291460
  1.7 8.4 %collective-permute-start = (bf16[8,4608]{1,0:T(8,128)(2,1)S(1)}, bf16[8,4608]{1,0:T(8,128)(2,1)S(1)}, u32[]{:S(2)}, u32[]{:S(2)}) collective-permute-start(bf16[8,4608]{1,0:T(8,128)(2,1)S(1)} %pad_maximum_fusion.1), channel_id=1, source_target_pairs={{0,1},{1,2},{2,3},{3,4},{4,5},{5,6},{6,7},{8,9},{9,10},{10,11},{11... | collective-permute-start | bytes 221192 | tf_op jit(solution)/shard_map/ppermute | solution.py:191
  35.1 48.0 %copy-start.3 = (f32[32,1024]{1,0:T(8,128)S(1)}, f32[32,1024]{1,0:T(8,128)}, u32[]{:S(2)}) copy-start(f32[32,1024]{1,0:T(8,128)} %get-tuple-element.19) | copy-start | bytes 393220
  35.1 48.7 %copy-start.5 = (f32[32]{0:T(128)S(1)}, f32[32]{0:T(128)}, u32[]{:S(2)}) copy-start(f32[32]{0:T(128)} %param.19) | copy-start | bytes 388
  35.2 36.3 %all-to-all-start = ((bf16[32,128,128]{2,1,0:T(8,128)(2,1)}), bf16[32,128,128]{2,1,0:T(8,128)(2,1)S(1)}, u32[]{:S(2)}, u32[]{:S(2)}) async-start(bf16[32,128,128]{2,1,0:T(8,128)(2,1)} %get-tuple-element.22), calls=%async_computation | async-start | bytes 2097152 | tf_op jit(solution)/shard_map/all_to_all | solution.py:249
  76.9 29.2 %all-to-all-start.1 = ((bf16[32,128,128]{2,1,0:T(8,128)(2,1)}), bf16[32,128,128]{2,1,0:T(8,128)(2,1)S(1)}, u32[]{:S(2)}, u32[]{:S(2)}) async-start(bf16[32,128,128]{2,1,0:T(8,128)(2,1)} %fusion.1), calls=%async_computation.1 | async-start | bytes 2097152 | tf_op jit(solution)/shard_map/all_to_all | solution.py:258
  101.1 32.5 %copy-start.4 = (f32[4096]{0:T(1024)S(1)}, f32[4096]{0:T(1024)}, u32[]{:S(2)}) copy-start(f32[4096]{0:T(1024)} %param.21) | copy-start | bytes 49156
  106.1 1.0 copy-start.2
  133.7 9.7 %copy-start.1 = (f32[32,128,128]{2,1,0:T(8,128)S(1)}, f32[32,128,128]{2,1,0:T(8,128)}, u32[]{:S(2)}) copy-start(f32[32,128,128]{2,1,0:T(8,128)} %param.20) | copy-start | bytes 6291460

commit v2 on v1

--- a/solution.py
+++ b/solution.py
@@ -11,6 +11,7 @@
 STEP_HEADS = 4
 LANES = 128
 LOG2E = 1.4426950408889634
+RELAY_FROM = 2
 norm_eps = 1e-05
 VMEM = 56 * 1024 * 1024
 f32 = jnp.float32
@@ -82,7 +83,7 @@
 
 
 def states_kernel(x_ref, rim_ref, taps_ref, cols_ref, dec_ref, bt_ref,
-                  xc_ref, starts_ref, sum_ref, halo_ref, turn_ref):
+                  xc_ref, starts_ref, sum_ref, fade_ref, halo_ref, turn_ref):
     rows = x_ref.shape[0]
     segments = rows // SPAN
     turn_ref[...] = turned(cols_ref[...])
@@ -114,21 +115,19 @@
         running = nxt
     for j in range(STEP_HEADS):
         sum_ref[j] = running[j].astype(sum_ref.dtype)
-
-
-def local_kernel(xc_ref, cols_ref, vrow_ref, c_ref, bt_ref, starts_ref, skip_ref,
-                 out_ref, turn_ref):
+        fade_ref[j] = jnp.broadcast_to(dec[segments : segments + 1, j : j + 1], (8, LANES))
+
+
+def inside(xc_ref, turn_ref, vrow_ref, c_ref, bt_ref, starts_ref, skip_ref, out_ref):
     rows = xc_ref.shape[0]
     segments = rows // SPAN
     half = SPAN // 2
-    turn_ref[...] = turned(cols_ref[...])
     r = lax.broadcasted_iota(jnp.int32, (half, half), 0)
     c = lax.broadcasted_iota(jnp.int32, (half, half), 1)
     causal = r >= c
     for k in range(segments):
         base = k * SPAN
         at = slice(base, base + SPAN)
-        top, low = slice(base, base + half), slice(base + half, base + SPAN)
         scores = dot(c_ref[at], bt_ref[:, at])
         s_tt = jnp.where(causal, scores[:half, :half], 0.0)
         s_lt = scores[half:, :half]
@@ -151,25 +150,168 @@
             out_ref[at, lanes] = y
 
 
-def gate_kernel(part_ref, z_ref, cols_ref, c_ref, inc_ref, out_ref, sq_ref):
-    cols = turned(cols_ref[...])
+def gate(part_ref, z_ref, turn_ref, c_ref, inc_ref, out_ref, sq_ref):
     rows = part_ref.shape[0]
-
-    @pl.when(pl.program_id(0) == 0)
-    def _():
-        sq_ref[...] = jnp.zeros_like(sq_ref)
-
     for k in range(rows // SPAN):
         at = slice(k * SPAN, (k + 1) * SPAN)
         total = sq_ref[at]
         for j in range(STEP_HEADS):
             lanes = slice(j * LANES, (j + 1) * LANES)
             carried = dot(c_ref[at], inc_ref[j])
-            mixed = part_ref[at, lanes] + cols[at, 96 + j : 97 + j] * carried
+            mixed = part_ref[at, lanes] + turn_ref[at, 96 + j : 97 + j] * carried
             gated = mixed * half_silu(z_ref[at, lanes].astype(f32) * 0.5)
             total = total + gated * gated
-            out_ref[at, lanes] = gated.astype(out_ref.dtype)
+            out_ref[at, lanes] = gated
         sq_ref[at] = total
+
+
+def mix_kernel(steps, peers, pairs, inner,
+               xc_ref, z_ref, cols_ref, vrow_ref, c_ref, bt_ref, starts_ref, skip_ref,
+               sum_ref, fade_ref, init_ref,
+               out_ref, inv_ref,
+               part_ref, turn_ref, sq_ref, near_ref, near_fade_ref, back_ref, ahead_ref,
+               give_ref, inc_ref, now_ref, rows_ref, got_ref,
+               near_send, near_recv, fade_send, fade_recv, chain_send, chain_recv,
+               give_send, give_recv, sq_send, sq_recv):
+    i = pl.program_id(0)
+    me = lax.axis_index("seq")
+    mine = lax.axis_index("head")
+    side = lax.rem(me, 2)
+    pair = me // 2
+    partner = me + 1 - 2 * side
+    chunks = steps // 2
+    own = side * chunks
+    other = chunks - own
+
+    def to_seq(src, dst, send, recv, target):
+        return pltpu.make_async_remote_copy(
+            src_ref=src, dst_ref=dst, send_sem=send, recv_sem=recv,
+            device_id={"seq": target}, device_id_type=pl.DeviceIdType.MESH)
+
+    def near(c):
+        return to_seq(sum_ref.at[pl.ds((other + c) * STEP_HEADS, STEP_HEADS)], near_ref.at[c],
+                      near_send.at[c], near_recv.at[c], partner)
+
+    def near_fade():
+        return to_seq(fade_ref.at[pl.ds(other * STEP_HEADS, chunks * STEP_HEADS)], near_fade_ref,
+                      fade_send, fade_recv, partner)
+
+    def chain(c, target):
+        return to_seq(ahead_ref.at[c], back_ref.at[c], chain_send.at[c], chain_recv.at[c], target)
+
+    def give(c):
+        return to_seq(give_ref.at[c], inc_ref.at[own + c], give_send.at[c], give_recv.at[c], partner)
+
+    def squares(p):
+        return pltpu.make_async_remote_copy(
+            src_ref=rows_ref, dst_ref=got_ref.at[p - 1], send_sem=sq_send.at[p - 1],
+            recv_sem=sq_recv.at[p - 1], device_id={"head": lax.rem(mine + p, peers)},
+            device_id_type=pl.DeviceIdType.MESH)
+
+    @pl.when(i == 0)
+    def _():
+        barrier = pltpu.get_barrier_semaphore()
+
+        def greet(**where):
+            pl.semaphore_signal(barrier, inc=1, device_id=where,
+                                device_id_type=pl.DeviceIdType.MESH)
+
+        greet(seq=partner)
+        for p in range(1, peers):
+            greet(head=lax.rem(mine + p, peers))
+
+        @pl.when(pair > 0)
+        def _():
+            greet(seq=me - 2)
+
+        @pl.when(pair < pairs - 1)
+        def _():
+            greet(seq=me + 2)
+
+        pl.semaphore_wait(
+            barrier, peers + jnp.minimum(pair, 1) + jnp.minimum(pairs - 1 - pair, 1))
+        near_fade().start()
+        for c in range(chunks):
+            near(c).start()
+        sq_ref[...] = jnp.zeros_like(sq_ref)
+
+    def relay(c):
+        if c == 0:
+            near_fade().wait_recv()
+        near(c).wait_recv()
+
+        @pl.when(pair == 0)
+        def _():
+            for j in range(STEP_HEADS):
+                now_ref[j] = init_ref[(own + c) * STEP_HEADS + j].T
+
+        @pl.when(pair > 0)
+        def _():
+            chain(c, partner).wait_recv()
+            now_ref[...] = back_ref[c].astype(f32)
+
+        for j in range(STEP_HEADS):
+            h = (own + c) * STEP_HEADS + j
+            here, there = sum_ref[h].astype(f32), near_ref[c, j].astype(f32)
+            d_here = fade_ref[h][0:1]
+            d_there = near_fade_ref[c * STEP_HEADS + j][0:1]
+            even = side == 0
+            first = now_ref[j]
+            second = (jnp.where(even, d_here, d_there) * first
+                      + jnp.where(even, here, there))
+            last = (jnp.where(even, d_there, d_here) * second
+                    + jnp.where(even, there, here))
+            inc_ref[own + c, j] = jnp.where(even, first, second).astype(bf16)
+            give_ref[c, j] = jnp.where(even, second, first).astype(bf16)
+            ahead_ref[c, j] = last.astype(bf16)
+
+        @pl.when(pair < pairs - 1)
+        def _():
+            chain(c, me + 2).start()
+
+        give(c).start()
+
+    for c in range(chunks):
+        pl.when(i == jnp.minimum(RELAY_FROM + c + pair, steps))(functools.partial(relay, c))
+
+    step = lax.rem(i, steps)
+    turn_ref[...] = pltpu.roll(cols_ref[...], lax.rem(LANES - step * STEP_HEADS, LANES), 1)
+
+    @pl.when(i < steps)
+    def _():
+        inside(xc_ref, turn_ref, vrow_ref, c_ref, bt_ref, starts_ref, skip_ref, part_ref.at[step])
+
+    @pl.when(i >= steps)
+    def _():
+        for c in range(chunks):
+            pl.when(step == other + c)(lambda c=c: give(c).wait_recv())
+        gate(part_ref.at[step], z_ref, turn_ref, c_ref, inc_ref.at[step], out_ref, sq_ref)
+
+    @pl.when(i == 2 * steps - 1)
+    def _():
+        count = rows_ref.shape[0]
+        for q in range(count):
+            rows_ref[q : q + 1] = jnp.sum(sq_ref[q * LANES : (q + 1) * LANES].T, axis=0,
+                                          keepdims=True)
+        for p in range(1, peers):
+            squares(p).start()
+        near_fade().wait_send()
+        for c in range(chunks):
+            near(c).wait_send()
+            give(c).wait_send()
+
+        @pl.when(pair < pairs - 1)
+        def _():
+            for c in range(chunks):
+                chain(c, partner).wait_send()
+
+        total = rows_ref[...]
+        for p in range(1, peers):
+            squares(p).wait_recv()
+            total = total + got_ref[p - 1]
+        inv_ref[...] = lax.rsqrt(total / inner + norm_eps)
+        for p in range(1, peers):
+            squares(p).wait_send()
 
 
 def local(x_input, bc_input, dt_input, z_gate, conv_x, conv_bc, dt_bias, a_log,
@@ -183,7 +325,6 @@
     width = STEP_HEADS * LANES
     segments = rows // SPAN
     n = lax.axis_size("seq")
-    me = lax.axis_index("seq")
     group_cols = bc_input.shape[2]
 
     tail = jnp.concatenate(
@@ -211,66 +352,76 @@
     whole = lambda shape: pl.BlockSpec(shape, lambda i: (0,) * len(shape))
     stripe = pl.BlockSpec((rows, width), lambda i: (0, i))
     bt_spec = pl.BlockSpec((state, rows), lambda i: (i // per_group, 0))
-    c_spec = pl.BlockSpec((rows, state), lambda i: (0, i // per_group))
     cols_spec = whole((rows, LANES))
     starts_spec = pl.BlockSpec((segments - 1, state, width), lambda i: (0, 0, i))
     heads_spec = pl.BlockSpec((STEP_HEADS, state, LANES), lambda i: (i, 0, 0))
-    x_conv, starts, summary = pl.pallas_call(
+    x_conv, starts, summary, fade = pl.pallas_call(
         states_kernel,
         grid=(steps,),
         in_specs=[stripe, pl.BlockSpec((8, width), lambda i: (0, i)),
                   pl.BlockSpec((4, width), lambda i: (0, i)), cols_spec, whole((8, LANES)), bt_spec],
-        out_specs=(stripe, starts_spec, heads_spec),
+        out_specs=(stripe, starts_spec, heads_spec,
+                   pl.BlockSpec((STEP_HEADS, 8, LANES), lambda i: (i, 0, 0))),
         out_shape=(
             jax.ShapeDtypeStruct((rows, channels), bf16),
             jax.ShapeDtypeStruct((segments - 1, state, channels), bf16),
             jax.ShapeDtypeStruct((heads, state, LANES), bf16),
+            jax.ShapeDtypeStruct((heads, 8, LANES), f32),
         ),
         scratch_shapes=[pltpu.VMEM((8, width), f32), pltpu.VMEM((rows, LANES), f32)],
         compiler_params=params(),
         name="states",
     )(x_input, x_rim, conv_x, cols, dec, b_t)
 
-    partial = pl.pallas_call(
-        local_kernel,
-        grid=(steps,),
-        in_specs=[stripe, cols_spec, pl.BlockSpec((1, STEP_HEADS, rows), lambda i: (i, 0, 0)),
-                  c_spec, bt_spec, starts_spec, pl.BlockSpec((1, width), lambda i: (0, i))],
-        out_specs=stripe,
-        out_shape=jax.ShapeDtypeStruct((rows, channels), f32),
-        scratch_shapes=[pltpu.VMEM((rows, LANES), f32)],
-        compiler_params=params(),
+    chunks = steps // 2
+    some = (chunks, STEP_HEADS, state, LANES)
+    peers = lax.axis_size("head")
+    now = lambda i: lax.rem(i, steps)
+    soon = lambda i: jnp.minimum(i, steps - 1)
+    late = lambda i: jnp.maximum(i - steps, 0)
+    dma = pltpu.SemaphoreType.DMA
+    gated, inverse = pl.pallas_call(
+        functools.partial(mix_kernel, steps, peers, n // 2, inner),
+        grid=(2 * steps,),
+        in_specs=[
+            pl.BlockSpec((rows, width), lambda i: (0, soon(i))),
+            pl.BlockSpec((rows, width), lambda i: (0, late(i))),
+            cols_spec,
+            pl.BlockSpec((1, STEP_HEADS, rows), lambda i: (soon(i), 0, 0)),
+            pl.BlockSpec((rows, state), lambda i: (0, now(i) // per_group)),
+            pl.BlockSpec((state, rows), lambda i: (soon(i) // per_group, 0)),
+            pl.BlockSpec((segments - 1, state, width), lambda i: (0, 0, soon(i))),
+            pl.BlockSpec((1, width), lambda i: (0, soon(i))),
+            whole((heads, state, LANES)),
+            whole((heads, 8, LANES)),
+            whole((heads, LANES, state)),
+        ],
+        out_specs=(pl.BlockSpec((rows, width), lambda i: (0, late(i))),
+                   whole((rows // LANES, LANES))),
+        out_shape=(jax.ShapeDtypeStruct((rows, channels), f32),
+                   jax.ShapeDtypeStruct((rows // LANES, LANES), f32)),
+        scratch_shapes=[
+            pltpu.VMEM((steps, rows, width), f32),
+            pltpu.VMEM((rows, LANES), f32),
+            pltpu.VMEM((rows, LANES), f32),
+            pltpu.VMEM(some, bf16),
+            pltpu.VMEM((heads // 2, 8, LANES), f32),
+            pltpu.VMEM(some, bf16),
+            pltpu.VMEM(some, bf16),
+            pltpu.VMEM(some, bf16),
+            pltpu.VMEM((steps, STEP_HEADS, state, LANES), bf16),
+            pltpu.VMEM((STEP_HEADS, state, LANES), f32),
+            pltpu.VMEM((rows // LANES, LANES), f32),
+            pltpu.VMEM((peers - 1, rows // LANES, LANES), f32),
+            dma((chunks,)), dma((chunks,)), dma, dma, dma((chunks,)), dma((chunks,)),
+            dma((chunks,)), dma((chunks,)), dma((peers - 1,)), dma((peers - 1,)),
+        ],
+        compiler_params=params(collective_id=0, has_side_effects=True),
         cost_estimate=pl.CostEstimate(flops=8 * 10**9, bytes_accessed=40 * 2**20, transcendentals=0),
-        name="inside",
-    )(x_conv, cols, vrow, c_mat, b_t, starts, jnp.repeat(d_skip, LANES)[None])
-
-    factor = lax.all_gather(dec[segments, :heads], "seq", axis=0)
-    share = heads // n
-    got = lax.all_to_all(summary, "seq", split_axis=0, concat_axis=0, tiled=True)
-    got = got.reshape(n, share, state, LANES).astype(f32)
-    mine = lax.dynamic_slice_in_dim(factor, me * share, share, 1)[:, :, None, None]
-    seed = lax.dynamic_slice_in_dim(init_state, me * share, share, 0).transpose(0, 2, 1)
-    running = seed
-    sent = []
-    for i in range(n):
-        sent.append(running.astype(bf16))
-        running = mine[i] * running + got[i]
-    incoming = lax.all_to_all(jnp.concatenate(sent, axis=0), "seq", split_axis=0, concat_axis=0,
-                              tiled=True)
-
-    gated, squares = pl.pallas_call(
-        gate_kernel,
-        grid=(steps,),
-        in_specs=[stripe, stripe, cols_spec, c_spec, heads_spec],
-        out_specs=(stripe, cols_spec),
-        out_shape=(jax.ShapeDtypeStruct((rows, channels), f32),
-                   jax.ShapeDtypeStruct((rows, LANES), f32)),
-        compiler_params=params(),
-        name="gate",
-    )(partial, z_gate, cols, c_mat, incoming)
-    total = lax.psum(jnp.sum(squares, axis=1), "head")
-    inverse = lax.rsqrt(total / inner + norm_eps)
-    return (gated * inverse[:, None] * norm_gain).astype(bf16)
+        name="mix",
+    )(x_conv, z_gate, cols, vrow, c_mat, b_t, starts, jnp.repeat(d_skip, LANES)[None],
+      summary, fade, init_state)
+    return (gated * inverse.reshape(rows, 1) * norm_gain).astype(bf16)
 
 
 def solution(mesh):

time: 144 us -> 95 us (0.66)
  the two profiles are of different devices: /device:TPU:0 before, /device:TPU:27 now
where the time goes in v2:
time: 95 us; the launch traced here: 94.4 us
  Pallas kernels  73 us (77%)
  other arithmetic  12.7 us (13%)
  local copies, waits for them, and re-layouts  5.5 us (6%)
  starting transfers between devices  3.15 us (3%)
    pallas_call x1, Pallas kernels, local(): pl.pallas_call(functools.partial(mix_kernel, steps, peers, n // 2, inner)...  49.1 us
    pallas_call x1, Pallas kernels, local(): pl.pallas_call(states_kernel, grid=(steps,), in_specs=[stripe, pl.BlockSp...  18.6 us
    convert_element_type x1, other arithmetic, local(): return (gated * inverse.reshape(rows, 1) * norm_gain).astype(bf16)  9.54 us
    pallas_call x1, Pallas kernels, local(): pl.pallas_call(prepare_kernel, out_shape=(jax.ShapeDtypeStruct((rows, LAN...  5.32 us
    ppermute x1, starting transfers between devices, local(): lax.ppermute(tail, 'seq', [(i, i + 1) for i in range(n - 1)]).astype(f32)  3.15 us
  transfers between devices with their start and end apart: 1, of which 0 were waited for; matrix products, arithmetic and copies ran while one was open for 4% of the time, Pallas kernels for 0%

profile of v2, /device:TPU:27, one launch (start us, length us, event | category | flops | bytes accessed | tf_op | source)
XLA Modules:
  0.0 94.4 jit_solution(2103028394115135890)
XLA Ops:
  0.0 0.0 copy-start.1
  0.0 0.7 slice_bitcast_fusion.3
  0.7 0.8 slice.18
  1.6 3.1 %collective-permute-start = (bf16[8,4608]{1,0:T(8,128)(2,1)S(1)}, bf16[8,4608]{1,0:T(8,128)(2,1)S(1)}, u32[]{:S(2)}, u32[]{:S(2)}) collective-permute-start(bf16[8,4608]{1,0:T(8,128)(2,1)S(1)} %pad_maximum_fusion.1), channel_id=1, source_target_pairs={{0,1},{1,2},{2,3},{3,4},{4,5},{5,6},{6,7},{8,9},{9,10},{10,11},{11... | collective-permute-start | bytes 221192 | tf_op jit(solution)/shard_map/ppermute | solution.py:332
  4.7 1.0 %copy.12 = bf16[1024,32]{1,0:T(8,128)(2,1)S(1)} copy(bf16[1024,32]{0,1:T(8,128)(2,1)} %param.13) | data formatting | bytes 131072 | tf_op args[2]
  5.7 1.0 %pad_maximum_fusion.dt_ref = bf16[1024,128]{1,0:T(8,128)(2,1)} fusion(bf16[1024,32]{1,0:T(8,128)(2,1)S(1)} %copy.12), kind=kLoop, calls=%fused_computation.1 | loop fusion | flops 1048576 | bytes 327680 | tf_op jit(solution)/shard_map/concatenate | solution.py:337
  6.8 1.5 %maximum_bitcast_fusion = (f32[1,128]{1,0:T(1,128)}, f32[1,128]{1,0:T(1,128)}) fusion(f32[32]{0:T(128)} %param.17, f32[32]{0:T(128)} %param.18), kind=kLoop, calls=%fused_computation.8 | loop fusion | flops 768 | bytes 1280 | tf_op jit(solution)/shard_map/broadcast_in_dim | solution.py:349
  8.2 0.0 collective-permute-done
  8.3 0.6 pad_maximum_fusion.2.rim_ref
  8.9 5.3 %prepare.1 = (f32[1024,128]{1,0:T(8,128)}, f32[32,1024]{1,0:T(8,128)}, f32[8,128]{1,0:T(8,128)}, bf16[1024,256]{1,0:T(8,128)(2,1)}, bf16[256,1024]{1,0:T(8,128)(2,1)}) custom-call(bf16[1024,128]{1,0:T(8,128)(2,1)} %pad_maximum_fusion.dt_ref, f32[1,128]{1,0:T(1,128)} %get-tuple-element.31.bias_ref, f32[1,128]{1,0:T(1,128)} %get-tuple-element.32.alog_ref, ...), custom_call_target="tpu_custom_call" | custom-call | tf_op jit(solution)/shard_map/prepare/pallas_call | solution.py:338
  14.2 1.6 %reshape.6.vrow_ref = f32[8,4,1024]{2,1,0:T(4,128)} reshape(f32[32,1024]{1,0:T(8,128)} %get-tuple-element.20) | data formatting | bytes 262144 | tf_op jit(solution)/shard_map/reshape | solution.py:350
  15.8 0.7 slice.24.rim_ref
  16.4 18.6 %states.1 = (bf16[1024,4096]{1,0:T(8,128)(2,1)}, bf16[3,128,4096]{2,1,0:T(8,128)(2,1)}, bf16[32,128,128]{2,1,0:T(8,128)(2,1)}, f32[32,8,128]{2,1,0:T(8,128)}) custom-call(bf16[1024,4096]{1,0:T(8,128)(2,1)} %x_ref.1, f32[8,4096]{1,0:T(8,128)} %slice.24.rim_ref, f32[4,4096]{1,0:T(4,128)} %taps_ref.3, f32[1024,128]{1,0:T(8,128)} %get-tuple-element.16.cols_ref, ...), custom_call_target="tpu_custom_call" | custom-call | tf_op jit(solution)/shard_map/states/pallas_call | solution.py:358
  35.1 0.0 copy-done.1
  35.1 0.7 broadcast_in_dim.12
  35.7 0.0 copy-start
  35.7 49.1 %mix.1 = (f32[1024,4096]{1,0:T(8,128)}, f32[8,128]{1,0:T(8,128)}) custom-call(bf16[1024,4096]{1,0:T(8,128)(2,1)} %get-tuple-element.19.xc_ref, bf16[1024,4096]{1,0:T(8,128)(2,1)} %z_ref.1, f32[1024,128]{1,0:T(8,128)} %get-tuple-element.16.cols_ref, f32[8,4,1024]{2,1,0:T(4,128)} %reshape.6.vrow_ref, bf16[1024,256]{1,0:T(8,128)(2,1)} %get-tuple-element.21.c_ref, ...), custom_call_target="tpu_custom_call" | custom-call | flops 8000000000 | bytes 41943040 | tf_op jit(solution)/shard_map/mix/pallas_call | solution.py:383
  84.8 0.0 copy-done
  84.8 9.5 %multiply_convert_fusion = bf16[1024,4096]{1,0:T(8,128)(2,1)} fusion(f32[1024,4096]{1,0:T(8,128)} %get-tuple-element.25, f32[4096]{0:T(1024)S(1)} %copy-done, f32[1024]{0:T(1024)} %bitcast.15), kind=kLoop, calls=%fused_computation | loop fusion | flops 12582912 | bytes 25186304 | tf_op jit(solution)/shard_map/convert_element_type | solution.py:424
  (3 shorter events, 0.0 us)
Async XLA Ops:
  0.0 35.1 %copy-start.1 = (f32[32]{0:T(128)S(1)}, f32[32]{0:T(128)}, u32[]{:S(2)}) copy-start(f32[32]{0:T(128)} %param.19) | copy-start | bytes 388
  1.6 6.7 %collective-permute-start = (bf16[8,4608]{1,0:T(8,128)(2,1)S(1)}, bf16[8,4608]{1,0:T(8,128)(2,1)S(1)}, u32[]{:S(2)}, u32[]{:S(2)}) collective-permute-start(bf16[8,4608]{1,0:T(8,128)(2,1)S(1)} %pad_maximum_fusion.1), channel_id=1, source_target_pairs={{0,1},{1,2},{2,3},{3,4},{4,5},{5,6},{6,7},{8,9},{9,10},{10,11},{11... | collective-permute-start | bytes 221192 | tf_op jit(solution)/shard_map/ppermute | solution.py:332
  35.7 49.1 %copy-start = (f32[4096]{0:T(1024)S(1)}, f32[4096]{0:T(1024)}, u32[]{:S(2)}) copy-start(f32[4096]{0:T(1024)} %param.21) | copy-start | bytes 49156

commit v3 on v2

--- a/solution.py
+++ b/solution.py
@@ -12,6 +12,7 @@
 LANES = 128
 LOG2E = 1.4426950408889634
 RELAY_FROM = 2
+RIM = 16
 norm_eps = 1e-05
 VMEM = 56 * 1024 * 1024
 f32 = jnp.float32
@@ -34,25 +35,67 @@
     return acc
 
 
-def prepare_kernel(dt_ref, bias_ref, alog_ref, bc_ref, rim_ref, taps_ref,
-                   cols_ref, vrow_ref, dec_ref, c_ref, bt_ref):
+def prepare_kernel(count, x_ref, dt_ref, bias_ref, alog_ref, bc_ref, taps_ref,
+                   cols_ref, vrow_ref, dec_ref, c_ref, bt_ref, x_rim_ref,
+                   x_got_ref, bc_got_ref, bc_rim_ref, x_send, x_recv, bc_send, bc_recv):
     rows = dt_ref.shape[0]
     segments = rows // SPAN
+    heads_here = dt_ref.shape[1]
+    me = lax.axis_index("seq")
+    barrier = pltpu.get_barrier_semaphore()
+
+    def to_next(src, dst, send, recv):
+        return pltpu.make_async_remote_copy(
+            src_ref=src, dst_ref=dst, send_sem=send, recv_sem=recv,
+            device_id={"seq": jnp.minimum(me + 1, count - 1)},
+            device_id_type=pl.DeviceIdType.MESH)
+
+    x_copy = to_next(x_ref.at[pl.ds(rows - RIM, RIM)], x_got_ref, x_send, x_recv)
+    bc_copy = to_next(bc_ref.at[:, pl.ds(rows - RIM, RIM)], bc_got_ref, bc_send, bc_recv)
+
+    @pl.when(me > 0)
+    def _():
+        pl.semaphore_signal(barrier, inc=1, device_id={"seq": me - 1},
+                            device_id_type=pl.DeviceIdType.MESH)
+
+    @pl.when(me < count - 1)
+    def _():
+        pl.semaphore_signal(barrier, inc=1, device_id={"seq": me + 1},
+                            device_id_type=pl.DeviceIdType.MESH)
+
+    pl.semaphore_wait(barrier, jnp.minimum(me, 1) + jnp.minimum(count - 1 - me, 1))
+
+    @pl.when(me < count - 1)
+    def _():
+        bc_copy.start()
+        x_copy.start()
+
+    rep = (lax.broadcasted_iota(jnp.int32, (heads_here, LANES), 0)
+           == lax.broadcasted_iota(jnp.int32, (heads_here, LANES), 1) % heads_here)
+    rep = rep.astype(f32)
+
+    def spread(row):
+        return jnp.dot(jnp.broadcast_to(row, (8, heads_here)), rep,
+                       precision=lax.Precision.HIGHEST, preferred_element_type=f32)[:1]
+
     r = lax.broadcasted_iota(jnp.int32, (SPAN, SPAN), 0)
     c = lax.broadcasted_iota(jnp.int32, (SPAN, SPAN), 1)
     tri = (r >= c).astype(f32)
     lane = lax.broadcasted_iota(jnp.int32, (SPAN, LANES), 1) // (LANES // 4)
-    rate = -jnp.exp(alog_ref[...]) * LOG2E
+    rate = -jnp.exp(spread(alog_ref[...])) * LOG2E
+    bias = spread(bias_ref[...])
     pre = jnp.zeros((1, LANES), f32)
     decays = []
     for k in range(segments):
         at = slice(k * SPAN, (k + 1) * SPAN)
-        v = dt_ref[at].astype(f32) + bias_ref[...]
+        v = dot(dt_ref[at], rep.astype(bf16)) + bias
         ts = jnp.maximum(v, 0.0) + jnp.log1p(jnp.exp(-jnp.abs(v)))
         cum = jnp.dot(tri, ts * rate, precision=lax.Precision.HIGHEST,
                       preferred_element_type=f32)
         end = cum[SPAN - 1 : SPAN]
-        vrow_ref[:, at] = (cum - jnp.log2(ts)).T[: LANES // 4]
+        v_rows = (cum - jnp.log2(ts)).T
+        for g in range(heads_here // STEP_HEADS):
+            vrow_ref[g, :, at] = v_rows[g * STEP_HEADS : (g + 1) * STEP_HEADS]
         tail = jnp.exp2(end - cum) * ts
         cols_ref[at] = jnp.where(
             lane == 0, cum,
@@ -63,9 +106,22 @@
     decays.append(jnp.exp2(pre))
     decays.append(jnp.zeros((8 - len(decays), LANES), f32))
     dec_ref[...] = jnp.concatenate(decays, axis=0)
+
+    @pl.when(me > 0)
+    def _():
+        bc_copy.wait_recv()
+        x_copy.wait_recv()
+        bc_rim_ref[...] = bc_got_ref[...].astype(f32)
+        x_rim_ref[...] = x_got_ref[...].astype(f32)
+
+    @pl.when(me == 0)
+    def _():
+        bc_rim_ref[...] = jnp.zeros_like(bc_rim_ref)
+        x_rim_ref[...] = jnp.zeros_like(x_rim_ref)
+
     for i in range(2):
         taps = taps_ref[i] * 0.5
-        halo = rim_ref[i]
+        halo = bc_rim_ref[i, RIM - 8 :]
         for k in range(segments):
             at = slice(k * SPAN, (k + 1) * SPAN)
             block = bc_ref[i, at].astype(f32)
@@ -76,6 +132,11 @@
             else:
                 c_ref[at] = out.astype(bf16)
 
+    @pl.when(me < count - 1)
+    def _():
+        bc_copy.wait_send()
+        x_copy.wait_send()
+
 
 def turned(ref_value, width=LANES):
     step = pl.program_id(0)
@@ -83,12 +144,11 @@
 
 
 def states_kernel(x_ref, rim_ref, taps_ref, cols_ref, dec_ref, bt_ref,
-                  xc_ref, starts_ref, sum_ref, fade_ref, halo_ref, turn_ref):
+                  xc_ref, starts_ref, sum_ref, fade_ref, turn_ref, shift_ref):
     rows = x_ref.shape[0]
     segments = rows // SPAN
     turn_ref[...] = turned(cols_ref[...])
     dec = turned(dec_ref[...])
-    halo_ref[...] = rim_ref[...]
     running = None
     for k in range(segments):
         at = slice(k * SPAN, (k + 1) * SPAN)
@@ -97,10 +157,17 @@
             lanes = slice(j * LANES, (j + 1) * LANES)
             block = x_ref[at, lanes].astype(f32)
             if k == 0:
-                halo = halo_ref[:, lanes]
+                halo = rim_ref[RIM - 8 :, lanes]
             else:
                 halo = x_ref[k * SPAN - 16 : k * SPAN, lanes].astype(f32)[8:]
-            xc = half_silu(conv_half(halo, block, taps_ref[:, lanes] * 0.5)).astype(bf16)
+            taps = taps_ref[:, lanes] * 0.5
+            shift = shift_ref.at[(k * STEP_HEADS + j) % 2]
+            shift[:8] = halo
+            shift[8:] = block
+            summed = block * taps[3:4]
+            for back in range(1, 4):
+                summed = summed + shift[8 - back : 8 - back + SPAN] * taps[3 - back : 4 - back]
+            xc = half_silu(summed).astype(bf16)
             xc_ref[at, lanes] = xc
             tail = turn_ref[at, 64 + j : 65 + j]
             weighted.append((xc.astype(f32) * tail).astype(bf16))
@@ -144,7 +211,7 @@
             x = xc_ref[at, lanes]
             y_t = dot(m_tt.astype(bf16), x[:half])
             y_l = dot(jnp.concatenate([m_lt, m_ll], axis=1).astype(bf16), x)
-            y = jnp.concatenate([y_t, y_l], axis=0) + skip_ref[:, lanes] * x.astype(f32)
+            y = jnp.concatenate([y_t, y_l], axis=0) + skip_ref[pl.program_id(0) * STEP_HEADS + j] * x.astype(f32)
             if k > 0:
                 y = y + turn_ref[at, 32 + j : 33 + j] * carried[:, lanes]
             out_ref[at, lanes] = y
@@ -152,13 +219,14 @@
 
 def gate(part_ref, z_ref, turn_ref, c_ref, inc_ref, out_ref, sq_ref):
     rows = part_ref.shape[0]
+    incoming = jnp.concatenate([inc_ref[j] for j in range(STEP_HEADS)], axis=1)
     for k in range(rows // SPAN):
         at = slice(k * SPAN, (k + 1) * SPAN)
         total = sq_ref[at]
+        carried = dot(c_ref[at], incoming)
         for j in range(STEP_HEADS):
             lanes = slice(j * LANES, (j + 1) * LANES)
-            carried = dot(c_ref[at], inc_ref[j])
-            mixed = part_ref[at, lanes] + turn_ref[at, 96 + j : 97 + j] * carried
+            mixed = part_ref[at, lanes] + turn_ref[at, 96 + j : 97 + j] * carried[:, lanes]
             gated = mixed * half_silu(z_ref[at, lanes].astype(f32) * 0.5)
             total = total + gated * gated
             out_ref[at, lanes] = gated
@@ -327,27 +395,27 @@
     n = lax.axis_size("seq")
     group_cols = bc_input.shape[2]
 
-    tail = jnp.concatenate(
-        [x_input[rows - 8 :], bc_input[0, rows - 8 :], bc_input[1, rows - 8 :]], axis=1)
-    rim = lax.ppermute(tail, "seq", [(i, i + 1) for i in range(n - 1)]).astype(f32)
-    x_rim = rim[:, :channels]
-    bc_rim = jnp.stack([rim[:, channels : channels + group_cols], rim[:, channels + group_cols :]])
-
     params = functools.partial(pltpu.CompilerParams, vmem_limit_bytes=VMEM)
-    four = lambda a: jnp.concatenate([a] * 4, axis=-1)
-    cols, vrow, dec, c_mat, b_t = pl.pallas_call(
-        prepare_kernel,
+    any_space = pl.BlockSpec(memory_space=pl.ANY)
+    in_vmem = pl.BlockSpec(memory_space=pltpu.VMEM)
+    dma = pltpu.SemaphoreType.DMA
+    cols, vrow, dec, c_mat, b_t, x_rim = pl.pallas_call(
+        functools.partial(prepare_kernel, n),
+        in_specs=[any_space] + [in_vmem] * 5,
+        out_specs=(in_vmem,) * 6,
         out_shape=(
             jax.ShapeDtypeStruct((rows, LANES), f32),
-            jax.ShapeDtypeStruct((heads, rows), f32),
+            jax.ShapeDtypeStruct((steps, STEP_HEADS, rows), f32),
             jax.ShapeDtypeStruct((8, LANES), f32),
             jax.ShapeDtypeStruct((rows, group_cols), bf16),
             jax.ShapeDtypeStruct((group_cols, rows), bf16),
+            jax.ShapeDtypeStruct((RIM, channels), f32),
         ),
-        compiler_params=params(),
+        scratch_shapes=[pltpu.VMEM((RIM, channels), bf16), pltpu.VMEM((2, RIM, group_cols), bf16),
+                        pltpu.VMEM((2, RIM, group_cols), f32), dma, dma, dma, dma],
+        compiler_params=params(collective_id=1, has_side_effects=True),
         name="prepare",
-    )(four(dt_input), four(dt_bias)[None], four(a_log)[None], bc_input, bc_rim, conv_bc)
-    vrow = vrow.reshape(steps, STEP_HEADS, rows)
+    )(x_input, dt_input, dt_bias[None], a_log[None], bc_input, conv_bc)
 
     whole = lambda shape: pl.BlockSpec(shape, lambda i: (0,) * len(shape))
     stripe = pl.BlockSpec((rows, width), lambda i: (0, i))
@@ -358,7 +426,7 @@
     x_conv, starts, summary, fade = pl.pallas_call(
         states_kernel,
         grid=(steps,),
-        in_specs=[stripe, pl.BlockSpec((8, width), lambda i: (0, i)),
+        in_specs=[stripe, pl.BlockSpec((RIM, width), lambda i: (0, i)),
                   pl.BlockSpec((4, width), lambda i: (0, i)), cols_spec, whole((8, LANES)), bt_spec],
         out_specs=(stripe, starts_spec, heads_spec,
                    pl.BlockSpec((STEP_HEADS, 8, LANES), lambda i: (i, 0, 0))),
@@ -368,7 +436,7 @@
             jax.ShapeDtypeStruct((heads, state, LANES), bf16),
             jax.ShapeDtypeStruct((heads, 8, LANES), f32),
         ),
-        scratch_shapes=[pltpu.VMEM((8, width), f32), pltpu.VMEM((rows, LANES), f32)],
+        scratch_shapes=[pltpu.VMEM((rows, LANES), f32), pltpu.VMEM((2, SPAN + 8, LANES), f32)],
         compiler_params=params(),
         name="states",
     )(x_input, x_rim, conv_x, cols, dec, b_t)
@@ -379,7 +447,6 @@
     now = lambda i: lax.rem(i, steps)
     soon = lambda i: jnp.minimum(i, steps - 1)
     late = lambda i: jnp.maximum(i - steps, 0)
-    dma = pltpu.SemaphoreType.DMA
     gated, inverse = pl.pallas_call(
         functools.partial(mix_kernel, steps, peers, n // 2, inner),
         grid=(2 * steps,),
@@ -391,7 +458,7 @@
             pl.BlockSpec((rows, state), lambda i: (0, now(i) // per_group)),
             pl.BlockSpec((state, rows), lambda i: (soon(i) // per_group, 0)),
             pl.BlockSpec((segments - 1, state, width), lambda i: (0, 0, soon(i))),
-            pl.BlockSpec((1, width), lambda i: (0, soon(i))),
+            pl.BlockSpec(memory_space=pltpu.SMEM),
             whole((heads, state, LANES)),
             whole((heads, 8, LANES)),
             whole((heads, LANES, state)),
@@ -419,7 +486,7 @@
         compiler_params=params(collective_id=0, has_side_effects=True),
         cost_estimate=pl.CostEstimate(flops=8 * 10**9, bytes_accessed=40 * 2**20, transcendentals=0),
         name="mix",
-    )(x_conv, z_gate, cols, vrow, c_mat, b_t, starts, jnp.repeat(d_skip, LANES)[None],
+    )(x_conv, z_gate, cols, vrow, c_mat, b_t, starts, d_skip,
       summary, fade, init_state)
     return (gated * inverse.reshape(rows, 1) * norm_gain).astype(bf16)
 

time: 95 us -> 88.2 us (0.928)
  local copies, waits for them, and re-layouts: 5.5 us -> 1.68 us
  Pallas kernels: 73 us -> 76.4 us
  other arithmetic: 12.7 us -> 9.54 us
  starting transfers between devices: 3.15 us -> 0 us
    pallas_call x1, Pallas kernels: 5.32 us -> 9.88 us  [local(): pl.pallas_call(functools.partial(prepare_kernel, n), in_specs=[any_space]...]
    ppermute x1 -> x0, starting transfers between devices: 3.15 us -> none  [local(): lax.ppermute(tail, 'seq', [(i, i + 1) for i in range(n - 1)]).astype(f32)]
    reshape x1 -> x0, local copies, waits for them, and re-layouts: 1.59 us -> none  [local(): vrow = vrow.reshape(steps, STEP_HEADS, rows)]
    slice x2 -> x0, local copies, waits for them, and re-layouts: 1.5 us -> none  [the longest x1 0.84 us: local(): x_input[rows - 8:]]
    broadcast_in_dim x1 -> x0, other arithmetic: 1.48 us -> none  [local(): four(dt_bias)[None]]
    concatenate x2 -> x0, other arithmetic: 1.02 us -> none  [the longest x1 1.02 us: local(): four = lambda a: jnp.concatenate([a] * 4, axis=-1)]
  transfers between devices with their start and end apart: 1 -> 0, of which waited for: 0 -> 0; matrix products, arithmetic and copies ran while one was open for 4% -> 0% of each run, Pallas kernels for 0% -> 0%
where the time goes in v3:
time: 88.2 us; the launch traced here: 87.7 us
  Pallas kernels  76.4 us (87%)
  other arithmetic  9.54 us (11%)
  local copies, waits for them, and re-layouts  1.68 us (2%)
    pallas_call x1, Pallas kernels, local(): pl.pallas_call(functools.partial(mix_kernel, steps, peers, n // 2, inner)...  48.8 us
    pallas_call x1, Pallas kernels, local(): pl.pallas_call(states_kernel, grid=(steps,), in_specs=[stripe, pl.BlockSp...  17.7 us
    pallas_call x1, Pallas kernels, local(): pl.pallas_call(functools.partial(prepare_kernel, n), in_specs=[any_space]...  9.88 us
    convert_element_type x1, other arithmetic, local(): return (gated * inverse.reshape(rows, 1) * norm_gain).astype(bf16)  9.54 us

profile of v3, /device:TPU:27, one launch (start us, length us, event | category | flops | bytes accessed | tf_op | source)
XLA Modules:
  0.0 87.7 jit_solution(15977787495977215507)
XLA Ops:
  0.0 1.7 %copy.12.dt_ref = bf16[1024,32]{1,0:T(8,128)(2,1)} copy(bf16[1024,32]{0,1:T(8,128)(2,1)} %param.13) | data formatting | bytes 131072 | tf_op args[2]
  1.7 9.9 %prepare.1 = (f32[1024,128]{1,0:T(8,128)}, f32[8,4,1024]{2,1,0:T(4,128)}, f32[8,128]{1,0:T(8,128)}, bf16[1024,256]{1,0:T(8,128)(2,1)}, bf16[256,1024]{1,0:T(8,128)(2,1)}, /*index=5*/f32[16,4096]{1,0:T(8,128)}) custom-call(bf16[1024,4096]{1,0:T(8,128)(2,1)} %x_ref.3, bf16[1024,32]{1,0:T(8,128)(2,1)} %copy.12.dt_ref, f32[1,32]{1,0:T(1,128)} %bitcast.4, ...), custom_call_target="tpu_custom_call" | custom-call | tf_op jit(solution)/shard_map/prepare/pallas_call | solution.py:402
  11.6 17.7 %states.1 = (bf16[1024,4096]{1,0:T(8,128)(2,1)}, bf16[3,128,4096]{2,1,0:T(8,128)(2,1)}, bf16[32,128,128]{2,1,0:T(8,128)(2,1)}, f32[32,8,128]{2,1,0:T(8,128)}) custom-call(bf16[1024,4096]{1,0:T(8,128)(2,1)} %x_ref.3, f32[16,4096]{1,0:T(8,128)} %get-tuple-element.17.rim_ref, f32[4,4096]{1,0:T(4,128)} %taps_ref.3, f32[1024,128]{1,0:T(8,128)} %get-tuple-element.18.cols_ref, ...), custom_call_target="tpu_custom_call" | custom-call | tf_op jit(solution)/shard_map/states/pallas_call | solution.py:426
  29.3 0.0 copy-start
  29.3 48.8 %mix.1 = (f32[1024,4096]{1,0:T(8,128)}, f32[8,128]{1,0:T(8,128)}) custom-call(bf16[1024,4096]{1,0:T(8,128)(2,1)} %get-tuple-element.21.xc_ref, bf16[1024,4096]{1,0:T(8,128)(2,1)} %z_ref.1, f32[1024,128]{1,0:T(8,128)} %get-tuple-element.18.cols_ref, f32[8,4,1024]{2,1,0:T(4,128)} %get-tuple-element.22.vrow_ref, bf16[1024,256]{1,0:T(8,128)(2,1)} %get-tuple-element.23.c_ref, ...), custom_call_target="tpu_custom_call" | custom-call | flops 8000000000 | bytes 41943040 | tf_op jit(solution)/shard_map/mix/pallas_call | solution.py:450
  78.1 0.0 copy-done
  78.1 9.5 %multiply_convert_fusion = bf16[1024,4096]{1,0:T(8,128)(2,1)} fusion(f32[1024,4096]{1,0:T(8,128)} %get-tuple-element.27, f32[4096]{0:T(1024)S(1)} %copy-done, f32[1024]{0:T(1024)} %bitcast.3), kind=kLoop, calls=%fused_computation | loop fusion | flops 12582912 | bytes 25186304 | tf_op jit(solution)/shard_map/convert_element_type | solution.py:491
Async XLA Ops:
  29.3 48.8 %copy-start = (f32[4096]{0:T(1024)S(1)}, f32[4096]{0:T(1024)}, u32[]{:S(2)}) copy-start(f32[4096]{0:T(1024)} %param.21) | copy-start | bytes 49156

commit v4 on v3

--- a/solution.py
+++ b/solution.py
@@ -233,6 +233,12 @@
         sq_ref[at] = total
 
 
+def turn_of(i, steps):
+    own = lax.rem(lax.axis_index("seq"), 2) * (steps // 2)
+    late = jnp.minimum(i // steps, 1)
+    return lax.rem(i + late * own, steps)
+
+
 def mix_kernel(steps, peers, pairs, inner,
                xc_ref, z_ref, cols_ref, vrow_ref, c_ref, bt_ref, starts_ref, skip_ref,
                sum_ref, fade_ref, init_ref,
@@ -340,9 +346,9 @@
         give(c).start()
 
     for c in range(chunks):
-        pl.when(i == jnp.minimum(RELAY_FROM + c + pair, steps))(functools.partial(relay, c))
-
-    step = lax.rem(i, steps)
+        pl.when(i == jnp.minimum(RELAY_FROM + c + 2 * pair, steps + c))(functools.partial(relay, c))
+
+    step = turn_of(i, steps)
     turn_ref[...] = pltpu.roll(cols_ref[...], lax.rem(LANES - step * STEP_HEADS, LANES), 1)
 
     @pl.when(i < steps)
@@ -444,9 +450,9 @@
     chunks = steps // 2
     some = (chunks, STEP_HEADS, state, LANES)
     peers = lax.axis_size("head")
-    now = lambda i: lax.rem(i, steps)
+    now = lambda i: turn_of(i, steps)
     soon = lambda i: jnp.minimum(i, steps - 1)
-    late = lambda i: jnp.maximum(i - steps, 0)
+    late = lambda i: turn_of(jnp.maximum(i, steps), steps)
     gated, inverse = pl.pallas_call(
         functools.partial(mix_kernel, steps, peers, n // 2, inner),
         grid=(2 * steps,),

time: 88.2 us -> 83.7 us (0.949)
  Pallas kernels: 76.4 us -> 71.9 us
    pallas_call x1, Pallas kernels: 48.8 us -> 44.3 us  [local(): pl.pallas_call(functools.partial(mix_kernel, steps, peers, n // 2, inner)...]
where the time goes in v4:
time: 83.7 us; the launch traced here: 83.1 us
  Pallas kernels  71.9 us (86%)
  other arithmetic  9.54 us (11%)
  local copies, waits for them, and re-layouts  1.68 us (2%)
    pallas_call x1, Pallas kernels, local(): pl.pallas_call(functools.partial(mix_kernel, steps, peers, n // 2, inner)...  44.3 us
    pallas_call x1, Pallas kernels, local(): pl.pallas_call(states_kernel, grid=(steps,), in_specs=[stripe, pl.BlockSp...  17.7 us
    pallas_call x1, Pallas kernels, local(): pl.pallas_call(functools.partial(prepare_kernel, n), in_specs=[any_space]...  9.88 us
    convert_element_type x1, other arithmetic, local(): return (gated * inverse.reshape(rows, 1) * norm_gain).astype(bf16)  9.54 us
    unnamed x3, local copies, waits for them, and re-layouts  1.68 us

profile of v4, /device:TPU:27, one launch (start us, length us, event | category | flops | bytes accessed | tf_op | source)
XLA Modules:
  0.0 83.1 jit_solution(16206140342264353525)
XLA Ops:
  0.0 1.7 %copy.12.dt_ref = bf16[1024,32]{1,0:T(8,128)(2,1)} copy(bf16[1024,32]{0,1:T(8,128)(2,1)} %param.13) | data formatting | bytes 131072 | tf_op args[2]
  1.7 9.9 %prepare.1 = (f32[1024,128]{1,0:T(8,128)}, f32[8,4,1024]{2,1,0:T(4,128)}, f32[8,128]{1,0:T(8,128)}, bf16[1024,256]{1,0:T(8,128)(2,1)}, bf16[256,1024]{1,0:T(8,128)(2,1)}, /*index=5*/f32[16,4096]{1,0:T(8,128)}) custom-call(bf16[1024,4096]{1,0:T(8,128)(2,1)} %x_ref.3, bf16[1024,32]{1,0:T(8,128)(2,1)} %copy.12.dt_ref, f32[1,32]{1,0:T(1,128)} %bitcast.4, ...), custom_call_target="tpu_custom_call" | custom-call | tf_op jit(solution)/shard_map/prepare/pallas_call | solution.py:408
  11.6 17.7 %states.1 = (bf16[1024,4096]{1,0:T(8,128)(2,1)}, bf16[3,128,4096]{2,1,0:T(8,128)(2,1)}, bf16[32,128,128]{2,1,0:T(8,128)(2,1)}, f32[32,8,128]{2,1,0:T(8,128)}) custom-call(bf16[1024,4096]{1,0:T(8,128)(2,1)} %x_ref.3, f32[16,4096]{1,0:T(8,128)} %get-tuple-element.17.rim_ref, f32[4,4096]{1,0:T(4,128)} %taps_ref.3, f32[1024,128]{1,0:T(8,128)} %get-tuple-element.18.cols_ref, ...), custom_call_target="tpu_custom_call" | custom-call | tf_op jit(solution)/shard_map/states/pallas_call | solution.py:432
  29.3 0.0 copy-start
  29.3 44.3 %mix.1 = (f32[1024,4096]{1,0:T(8,128)}, f32[8,128]{1,0:T(8,128)}) custom-call(bf16[1024,4096]{1,0:T(8,128)(2,1)} %get-tuple-element.21.xc_ref, bf16[1024,4096]{1,0:T(8,128)(2,1)} %z_ref.1, f32[1024,128]{1,0:T(8,128)} %get-tuple-element.18.cols_ref, f32[8,4,1024]{2,1,0:T(4,128)} %get-tuple-element.22.vrow_ref, bf16[1024,256]{1,0:T(8,128)(2,1)} %get-tuple-element.23.c_ref, ...), custom_call_target="tpu_custom_call" | custom-call | flops 8000000000 | bytes 41943040 | tf_op jit(solution)/shard_map/mix/pallas_call | solution.py:456
  73.6 0.0 copy-done
  73.6 9.5 %multiply_convert_fusion = bf16[1024,4096]{1,0:T(8,128)(2,1)} fusion(f32[1024,4096]{1,0:T(8,128)} %get-tuple-element.27, f32[4096]{0:T(1024)S(1)} %copy-done, f32[1024]{0:T(1024)} %bitcast.3), kind=kLoop, calls=%fused_computation | loop fusion | flops 12582912 | bytes 25186304 | tf_op jit(solution)/shard_map/convert_element_type | solution.py:497
Async XLA Ops:
  29.3 44.3 %copy-start = (f32[4096]{0:T(1024)S(1)}, f32[4096]{0:T(1024)}, u32[]{:S(2)}) copy-start(f32[4096]{0:T(1024)} %param.21) | copy-start | bytes 49156
